TPU v7x, 32 devices: a whole 2x2x4 slice. The times are simulated.
32 devices in a mesh: seq: 8 (over y, x, core), chan: 4 (over z).
Axes of the slice: x: 2, y: 2, z: 4, core: 2. Of those that a mesh axis runs over, the one named last changes fastest.
Arguments:
- doc_ids: int32 [2048], replicated, may hold values from 0 to 3, never falling along the last dimension, each value on 1 to 1024 neighbouring positions
- attn_queries: bfloat16 [2048, 8192], P(('seq', 'chan')), may hold values from -6 to 6
- attn_keys: bfloat16 [2048, 8192], P(('seq', 'chan')), may hold values from -6 to 6
- attn_values: bfloat16 [2048, 8192], P(('seq', 'chan')), may hold values from -6 to 6
- attn_cot: bfloat16 [2048, 8192], P(('seq', 'chan')), may hold values from -6 to 6
Outputs:
- attn_out: bfloat16 [2048, 8192], P('seq', 'chan')
- query_grad: bfloat16 [2048, 8192], P('seq', 'chan')
- key_grad: bfloat16 [2048, 8192], P('seq', 'chan')
- value_grad: bfloat16 [2048, 8192], P('seq', 'chan')
Inputs may be any that keep to these rules, and one draw needn't show every extreme that they name: `doc_ids`: documents are runs of equal ids that never fall; each holds 1 to 1024 tokens and one holds exactly 1024.
All inputs are finite; a program needn't handle non-finite values.
Results may differ from a plain program's by a relative error of at most 0.03.
Values may be sent and summed in bfloat16 or wider, within the bound.
No kernel may reach another device: no remote copies, remote signals or barrier semaphores. Data moves between devices by JAX's collectives and lax.ppermute only.
A program may use at most 256 MiB of HBM per device.

v0:
```python
import functools
import math

import jax
import jax.numpy as jnp
from jax import lax
from jax.experimental import pallas as pl
from jax.experimental.pallas import tpu as pltpu
from jax.sharding import PartitionSpec as P

HEAD_DIM = 128
DOC_MAX = 1024
NEG = -1e30
SCALE = HEAD_DIM ** (-0.5)
EXP_SCALE = SCALE * math.log2(math.e)
SCALARS = pl.BlockSpec(memory_space=pltpu.SMEM)
VECTORS = pl.BlockSpec(memory_space=pltpu.VMEM)
ANYWHERE = pl.BlockSpec(memory_space=pl.ANY)


def low_array(*shape):
    return jax.ShapeDtypeStruct(shape, jnp.bfloat16)


def moved(byte_count):
    return pl.CostEstimate(flops=0, bytes_accessed=byte_count, transcendentals=0)


def dot_nt(a, b):
    return lax.dot_general(a, b, (((1,), (1,)), ((), ())), preferred_element_type=jnp.float32)


def dot_nn(a, b):
    return lax.dot_general(a, b, (((1,), (0,)), ((), ())), preferred_element_type=jnp.float32)


def dot_tn(a, b):
    return lax.dot_general(a, b, (((0,), (0,)), ((), ())), preferred_element_type=jnp.float32)


def pack_kernel(owners, *refs):
    ins, out_ref = refs[:4], refs[4]
    for owner in range(owners):
        for which in range(4):
            out_ref[owner, 0, which] = ins[which][:, owner * HEAD_DIM : (owner + 1) * HEAD_DIM]


def pack(inputs, chans, turns, turn):
    rows, width = inputs[0].shape
    owners = width // HEAD_DIM // chans // turns
    return pl.pallas_call(
        functools.partial(pack_kernel, owners),
        grid=(chans, 2),
        out_shape=low_array(owners, chans, 4, rows, HEAD_DIM),
        in_specs=[pl.BlockSpec((rows // 2, owners * HEAD_DIM), lambda c, r: (r, c * turns + turn))]
        * 4,
        out_specs=pl.BlockSpec((owners, 1, 4, rows // 2, HEAD_DIM), lambda c, r: (0, c, 0, r, 0)),
        cost_estimate=moved(16 * rows * width // turns),
    )(*inputs)


def attention_kernel(spans, count_ref, start_ref, target_ref, in_ref, *refs):
    outs, (mixed_ref, key_acc, value_acc) = refs[:-3], refs[-3:]
    blocks, _, block, _ = mixed_ref.shape
    key_acc[...] = jnp.zeros_like(key_acc)
    value_acc[...] = jnp.zeros_like(value_acc)

    def tokens(which, first, count):
        return in_ref[pl.ds(first, count), :, which].reshape(count * block, HEAD_DIM)

    def work(i, span):
        low = i - (span - 1)
        width = span * block
        query = tokens(0, i, 1)
        cot = tokens(3, i, 1).astype(jnp.float32)
        key = tokens(1, low, span)
        value = tokens(2, low, span)
        start = start_ref[pl.ds(pl.multiple_of(i * block, block), block), :] - low * block
        col = lax.broadcasted_iota(jnp.int32, (block, width), 1)
        row = lax.broadcasted_iota(jnp.int32, (block, width), 0) + (span - 1) * block
        allowed = (col >= start) & (col <= row)
        score = jnp.where(allowed, dot_nt(query, key), NEG)
        peak = jnp.max(score, axis=1, keepdims=True)
        expo = jnp.exp2((score - peak) * EXP_SCALE)
        inverse = 1.0 / jnp.sum(expo, axis=1, keepdims=True)
        expo_low = expo.astype(jnp.bfloat16)
        mixed = dot_nn(expo_low, value) * inverse
        scaled = cot * inverse
        scaled_low = scaled.astype(jnp.bfloat16)
        rowdot = jnp.sum(mixed * scaled, axis=1, keepdims=True)
        dscore = (expo * (dot_nt(scaled_low, value) - rowdot)).astype(jnp.bfloat16)
        mixed_ref[i, 0] = mixed.astype(jnp.bfloat16)
        mixed_ref[i, 1] = (SCALE * dot_nn(dscore, key)).astype(jnp.bfloat16)
        held = pl.ds(pl.multiple_of(low * block, block), width)
        key_acc[held, :] += dot_tn(dscore, query)
        value_acc[held, :] += dot_tn(expo_low, scaled_low)

    def step(i, carry):
        for span in range(1, spans + 1):
            pl.when(count_ref[i] == span)(functools.partial(work, i, span))
        return carry

    lax.fori_loop(0, blocks, step, 0)
    for d, out_ref in enumerate(outs):
        i = target_ref[d]
        held = pl.ds(pl.multiple_of(i * block, block), block)
        out_ref[:2] = mixed_ref[i]
        out_ref[2] = (SCALE * key_acc[held, :]).astype(jnp.bfloat16)
        out_ref[3] = value_acc[held, :].astype(jnp.bfloat16)


def attention(count, start, targets, packed):
    shards, chans, _, rows, _ = packed.shape
    block = chans * rows
    total = shards * block
    spans = min(shards, (DOC_MAX + block - 2) // block + 1)
    pairs = total * block * min(spans, 3)
    return pl.pallas_call(
        functools.partial(attention_kernel, spans),
        out_shape=[low_array(4, block, HEAD_DIM)] * shards,
        in_specs=[SCALARS, VECTORS, SCALARS, VECTORS],
        out_specs=[VECTORS] * shards,
        scratch_shapes=[
            pltpu.VMEM((shards, 2, block, HEAD_DIM), jnp.bfloat16),
            pltpu.VMEM((total, HEAD_DIM), jnp.float32),
            pltpu.VMEM((total, HEAD_DIM), jnp.float32),
        ],
        compiler_params=pltpu.CompilerParams(vmem_limit_bytes=(10 << 20) + 3072 * total),
        cost_estimate=pl.CostEstimate(
            flops=12 * HEAD_DIM * pairs, bytes_accessed=16 * total * HEAD_DIM, transcendentals=pairs
        ),
    )(count, start, targets, packed)


def unpack_kernel(peers, base, shard_ref, *refs):
    blocks, outs, sems = refs[: len(peers)], refs[-5:-1], refs[-1]
    moves = []
    for b, d in enumerate(peers):
        head = base + jnp.bitwise_xor(shard_ref[0], d)
        columns = pl.ds(pl.multiple_of(head * HEAD_DIM, HEAD_DIM), HEAD_DIM)
        for which in range(4):
            moves.append(
                pltpu.make_async_copy(
                    blocks[b].at[which], outs[which].at[:, columns], sems.at[b, which]
                )
            )
    for move in moves:
        move.start()
    for move in moves:
        move.wait()


def unpack(shard, blocks, peers, base, width, held):
    count = len(blocks)
    rows = blocks[0].shape[1]
    return pl.pallas_call(
        functools.partial(unpack_kernel, peers, base),
        out_shape=[low_array(rows, width)] * 4,
        in_specs=[SCALARS] + [VECTORS] * count + [ANYWHERE] * len(held),
        out_specs=[ANYWHERE] * 4,
        scratch_shapes=[pltpu.SemaphoreType.DMA((count, 4))],
        input_output_aliases={1 + count + i: i for i in range(len(held))},
        compiler_params=pltpu.CompilerParams(vmem_limit_bytes=8 << 20),
        cost_estimate=moved(16 * count * rows * HEAD_DIM),
    )(shard, *blocks, *held)


def exchange(value, d):
    return lax.ppermute(value, "seq", [(s, s ^ d) for s in range(lax.axis_size("seq"))])


def on_device(doc_ids, *inputs):
    shards = lax.axis_size("seq")
    chans = lax.axis_size("chan")
    rows, width = inputs[0].shape
    heads = width // HEAD_DIM // chans
    turns = max(1, heads // shards)
    owners = heads // turns
    copies = shards // owners
    block = rows * chans
    start = jnp.sum((doc_ids[None, :] < doc_ids[:, None]).astype(jnp.int32), axis=1)
    count = jnp.arange(shards, dtype=jnp.int32) - start[::block] // block + 1
    start = start[:, None]
    peers = jnp.bitwise_xor(lax.axis_index("seq"), jnp.arange(shards, dtype=jnp.int32))
    tied = lax.optimization_barrier

    def gather(parts):
        parts = jnp.repeat(parts, copies, axis=0) if copies > 1 else parts
        parts = parts.reshape(shards * chans, 4, rows, HEAD_DIM)
        parts = lax.all_to_all(parts, ("seq", "chan"), split_axis=0, concat_axis=0, tiled=True)
        return parts.reshape(shards, chans, 4, rows, HEAD_DIM)

    parts = [pack(inputs, chans, turns, turn) for turn in range(turns)]
    later, count, start = tied((parts[1:], count, start))
    mine, parts = tied((gather(parts[0]), later))
    order = [0] + sorted(range(1, shards), key=lambda d: (-(d >> 1).bit_count(), d & 1, d))
    outs, blocks = (), ()
    for turn in range(turns):
        following = gather(parts[turn]) if turn + 1 < turns else None
        mine, blocks = tied((mine, blocks))
        if turn > 0:
            outs = unpack(place, blocks, order, (turn - 1) * owners, heads * HEAD_DIM, outs)
        blocks = list(attention(count, start, peers, mine))
        if copies == 1:
            blocks = [exchange(blocks[d], d) if d else blocks[d] for d in order]
            place = lax.axis_index("seq")[None]
        else:
            whole = jnp.stack(blocks)[peers]
            whole = lax.all_to_all(whole, "seq", split_axis=0, concat_axis=0, tiled=True)
            blocks = [whole[owner * copies] for owner in range(owners)]
            place, order = jnp.zeros((1,), jnp.int32), list(range(owners))
        mine = following
    early, base = len(blocks) // 2 + 1, (turns - 1) * owners
    outs = unpack(place, blocks[:early], order[:early], base, heads * HEAD_DIM, outs)
    return tuple(unpack(place, blocks[early:], order[early:], base, heads * HEAD_DIM, outs))


def solution(mesh):
    spread = P(("seq", "chan"), None)
    in_specs = (P(), spread, spread, spread, spread)
    out_specs = (P("seq", "chan"),) * 4
    return jax.shard_map(
        on_device, mesh=mesh, in_specs=in_specs, out_specs=out_specs, check_vma=False
    )
```

profile of v0, /device:TPU:9, one launch (start us, length us, event | category | flops | bytes accessed | tf_op | source)
XLA Modules:
  0.0 155.7 jit_solution(755542969933935060)
XLA Ops:
  0.6 5.8 %shard_map.85 = bf16[8,4,4,64,128]{4,3,2,1,0:T(8,128)(2,1)} custom-call(bf16[64,8192]{1,0:T(8,128)(2,1)} %refs_0_.3, bf16[64,8192]{1,0:T(8,128)(2,1)} %refs_1_.3, bf16[64,8192]{1,0:T(8,128)(2,1)} %refs_2_.3, bf16[64,8192]{1,0:T(8,128)(2,1)} %refs_3_.3), custom_call_target="tpu_custom_call" | custom-call | bytes 4194304 | tf_op jit(solution)/shard_map/pallas_call | solution.py:51
  6.5 6.4 %all-to-all-start = ((bf16[32,4,64,128]{3,2,1,0:T(8,128)(2,1)}), bf16[32,4,64,128]{3,2,1,0:T(8,128)(2,1)S(1)}, u32[]{:S(2)}, u32[]{:S(2)}) async-start(bf16[32,4,64,128]{3,2,1,0:T(8,128)(2,1)} %bitcast.9), calls=%async_computation | async-start | bytes 4194304 | tf_op jit(solution)/shard_map/all_to_all | solution.py:190
  12.9 5.8 %shard_map.84 = bf16[8,4,4,64,128]{4,3,2,1,0:T(8,128)(2,1)} custom-call(bf16[64,8192]{1,0:T(8,128)(2,1)} %refs_0_.3, bf16[64,8192]{1,0:T(8,128)(2,1)} %refs_1_.3, bf16[64,8192]{1,0:T(8,128)(2,1)} %refs_2_.3, bf16[64,8192]{1,0:T(8,128)(2,1)} %refs_3_.3), custom_call_target="tpu_custom_call" | custom-call | bytes 4194304 | tf_op jit(solution)/shard_map/pallas_call | solution.py:51
  18.7 1.8 %convert_reduce_fusion = s32[2048]{0:T(1024)S(1)} fusion(s32[2048]{0:T(1024)S(1)} %copy-done.16), kind=kLoop, calls=%fused_computation | loop fusion | flops 12580864 | bytes 16384 | tf_op jit(solution)/shard_map/reduce_sum | solution.py:181
  20.6 40.4 %all-to-all-done = bf16[32,4,64,128]{3,2,1,0:T(8,128)(2,1)S(1)} async-done(((bf16[32,4,64,128]{3,2,1,0:T(8,128)(2,1)}), bf16[32,4,64,128]{3,2,1,0:T(8,128)(2,1)S(1)}, u32[]{:S(2)}, u32[]{:S(2)}) %all-to-all-start) | async-done | bytes 2097184 | tf_op jit(solution)/shard_map/all_to_all | solution.py:190
  61.0 1.3 copy-done
  62.3 3.5 %all-to-all-start.1 = ((bf16[32,4,64,128]{3,2,1,0:T(8,128)(2,1)}), bf16[32,4,64,128]{3,2,1,0:T(8,128)(2,1)S(1)}, u32[]{:S(2)}, u32[]{:S(2)}) async-start(bf16[32,4,64,128]{3,2,1,0:T(8,128)(2,1)} %bitcast.8), calls=%async_computation.1 | async-start | bytes 4194304 | tf_op jit(solution)/shard_map/all_to_all | solution.py:190
  66.2 1.6 %copy-done.1 = bf16[32,4,64,128]{3,2,1,0:T(8,128)(2,1)S(1)} copy-done((bf16[32,4,64,128]{3,2,1,0:T(8,128)(2,1)S(1)}, bf16[32,4,64,128]{3,2,1,0:T(8,128)(2,1)}, u32[]{:S(2)}) %copy-start.1) | copy-done | bytes 2097176
  67.8 9.7 %shard_map.86 = (bf16[4,256,128]{2,1,0:T(8,128)(2,1)S(1)}, bf16[4,256,128]{2,1,0:T(8,128)(2,1)S(1)}, bf16[4,256,128]{2,1,0:T(8,128)(2,1)S(1)}, bf16[4,256,128]{2...) custom-call(s32[8]{0:T(128)S(1)} %subtract_add_fusion.count_ref, ...), custom_call_target="tpu_custom_call" | custom-call | flops 2415919104 | bytes 4194304 | tf_op jit(solution)/shard_map/pallas_call | solution.py:118
  77.5 2.1 %collective-permute-start = (bf16[4,256,128]{2,1,0:T(8,128)(2,1)S(1)}, bf16[4,256,128]{2,1,0:T(8,128)(2,1)S(1)}, u32[]{:S(2)}, u32[]{:S(2)}) collective-permute-start(bf16[4,256,128]{2,1,0:T(8,128)(2,1)S(1)} %get-tuple-element.48), channel_id=1, source_target_pairs={{0,24},{4,28},{8,16},{12,20},{16,8},{20,12},{24,0},{28,4},{1,25},{... | collective-permute-start | bytes 786440 | tf_op jit(solution)/shard_map/ppermute | solution.py:169
  79.7 0.8 collective-permute-start.1
  80.5 1.2 collective-permute-start.2
  81.7 1.2 collective-permute-start.3
  83.5 6.5 %collective-permute-done.refs_1_ = bf16[4,256,128]{2,1,0:T(8,128)(2,1)S(1)} collective-permute-done((bf16[4,256,128]{2,1,0:T(8,128)(2,1)S(1)}, bf16[4,256,128]{2,1,0:T(8,128)(2,1)S(1)}, u32[]{:S(2)}, u32[]{:S(2)}) %collective-permute-start) | collective-permute-done | bytes 262176 | tf_op jit(solution)/shard_map/ppermute | solution.py:169
  90.6 3.8 %collective-permute-start.5 = (bf16[4,256,128]{2,1,0:T(8,128)(2,1)S(1)}, bf16[4,256,128]{2,1,0:T(8,128)(2,1)S(1)}, u32[]{:S(2)}, u32[]{:S(2)}) collective-permute-start(bf16[4,256,128]{2,1,0:T(8,128)(2,1)S(1)} %get-tuple-element.53), channel_id=1, source_target_pairs={{0,20},{4,16},{8,28},{12,24},{16,4},{20,0},{24,12},{28,8},{1,21},{... | collective-permute-start | bytes 786440 | tf_op jit(solution)/shard_map/ppermute | solution.py:169
  94.4 9.9 %collective-permute-done.1.refs_2_ = bf16[4,256,128]{2,1,0:T(8,128)(2,1)S(1)} collective-permute-done((bf16[4,256,128]{2,1,0:T(8,128)(2,1)S(1)}, bf16[4,256,128]{2,1,0:T(8,128)(2,1)S(1)}, u32[]{:S(2)}, u32[]{:S(2)}) %collective-permute-start.1) | collective-permute-done | bytes 262176 | tf_op jit(solution)/shard_map/ppermute | solution.py:169
  105.1 5.1 %collective-permute-done.2.refs_3_ = bf16[4,256,128]{2,1,0:T(8,128)(2,1)S(1)} collective-permute-done((bf16[4,256,128]{2,1,0:T(8,128)(2,1)S(1)}, bf16[4,256,128]{2,1,0:T(8,128)(2,1)S(1)}, u32[]{:S(2)}, u32[]{:S(2)}) %collective-permute-start.2) | collective-permute-done | bytes 262176 | tf_op jit(solution)/shard_map/ppermute | solution.py:169
  111.6 5.0 %collective-permute-done.4.refs_5_ = bf16[4,256,128]{2,1,0:T(8,128)(2,1)S(1)} collective-permute-done((bf16[4,256,128]{2,1,0:T(8,128)(2,1)S(1)}, bf16[4,256,128]{2,1,0:T(8,128)(2,1)S(1)}, u32[]{:S(2)}, u32[]{:S(2)}) %collective-permute-start.4) | collective-permute-done | bytes 262176 | tf_op jit(solution)/shard_map/ppermute | solution.py:169
  118.8 9.7 %shard_map.87 = (bf16[4,256,128]{2,1,0:T(8,128)(2,1)S(1)}, bf16[4,256,128]{2,1,0:T(8,128)(2,1)S(1)}, bf16[4,256,128]{2,1,0:T(8,128)(2,1)S(1)}, bf16[4,256,128]{2...) custom-call(s32[8]{0:T(128)S(1)} %subtract_add_fusion.count_ref, ...), custom_call_target="tpu_custom_call" | custom-call | flops 2415919104 | bytes 4194304 | tf_op jit(solution)/shard_map/pallas_call | solution.py:118
  128.5 2.0 %collective-permute-start.10 = (bf16[4,256,128]{2,1,0:T(8,128)(2,1)S(1)}, bf16[4,256,128]{2,1,0:T(8,128)(2,1)S(1)}, u32[]{:S(2)}, u32[]{:S(2)}) collective-permute-start(bf16[4,256,128]{2,1,0:T(8,128)(2,1)S(1)} %get-tuple-element.60), channel_id=1, source_target_pairs={{0,24},{4,28},{8,16},{12,20},{16,8},{20,12},{24,0},{28,4},{1,25},{... | collective-permute-start | bytes 786440 | tf_op jit(solution)/shard_map/ppermute | solution.py:169
  130.5 0.9 collective-permute-start.11
  131.4 1.0 collective-permute-start.12
  132.5 0.9 collective-permute-start.13
  133.9 3.3 %collective-permute-done.10.refs_1_ = bf16[4,256,128]{2,1,0:T(8,128)(2,1)S(1)} collective-permute-done((bf16[4,256,128]{2,1,0:T(8,128)(2,1)S(1)}, bf16[4,256,128]{2,1,0:T(8,128)(2,1)S(1)}, u32[]{:S(2)}, u32[]{:S(2)}) %collective-permute-start.10) | collective-permute-done | bytes 262176 | tf_op jit(solution)/shard_map/ppermute | solution.py:169
  137.1 2.2 %collective-permute-start.8 = (bf16[4,256,128]{2,1,0:T(8,128)(2,1)S(1)}, bf16[4,256,128]{2,1,0:T(8,128)(2,1)S(1)}, u32[]{:S(2)}, u32[]{:S(2)}) collective-permute-start(bf16[4,256,128]{2,1,0:T(8,128)(2,1)S(1)} %get-tuple-element.57), channel_id=1, source_target_pairs={{0,20},{4,16},{8,28},{12,24},{16,4},{20,0},{24,12},{28,8},{1,21},{... | collective-permute-start | bytes 786440 | tf_op jit(solution)/shard_map/ppermute | solution.py:169
  139.3 4.6 %collective-permute-done.11.refs_2_ = bf16[4,256,128]{2,1,0:T(8,128)(2,1)S(1)} collective-permute-done((bf16[4,256,128]{2,1,0:T(8,128)(2,1)S(1)}, bf16[4,256,128]{2,1,0:T(8,128)(2,1)S(1)}, u32[]{:S(2)}, u32[]{:S(2)}) %collective-permute-start.11) | collective-permute-done | bytes 262176 | tf_op jit(solution)/shard_map/ppermute | solution.py:169
  144.0 1.6 %shard_map.88 = (bf16[256,2048]{1,0:T(8,128)(2,1)}, bf16[256,2048]{1,0:T(8,128)(2,1)}, bf16[256,2048]{1,0:T(8,128)(2,1)}, bf16[256,2048]{1,0:T(8,128)(2,1)}) custom-call(s32[1]{0:T(128)} %bitcast.shard_ref, bf16[4,256,128]{2,1,0:T(8,128)(2,1)S(1)} %get-tuple-element.64.refs_0_, bf16[4,256,128]{2,1,0:T(8,128)(2,1)S(1)} %copy-done.3, ...), custom_call_target="tpu_custom_call" | custom-call | bytes 4194304 | tf_op jit(solution)/shard_map/pallas_call | solution.py:156
  145.6 2.4 %collective-permute-done.12.refs_3_ = bf16[4,256,128]{2,1,0:T(8,128)(2,1)S(1)} collective-permute-done((bf16[4,256,128]{2,1,0:T(8,128)(2,1)S(1)}, bf16[4,256,128]{2,1,0:T(8,128)(2,1)S(1)}, u32[]{:S(2)}, u32[]{:S(2)}) %collective-permute-start.12) | collective-permute-done | bytes 262176 | tf_op jit(solution)/shard_map/ppermute | solution.py:169
  147.9 1.1 collective-permute-done.13.refs_4_
  149.0 1.2 shard_map.89
  150.2 3.9 %collective-permute-done.7.refs_0_ = bf16[4,256,128]{2,1,0:T(8,128)(2,1)S(1)} collective-permute-done((bf16[4,256,128]{2,1,0:T(8,128)(2,1)S(1)}, bf16[4,256,128]{2,1,0:T(8,128)(2,1)S(1)}, u32[]{:S(2)}, u32[]{:S(2)}) %collective-permute-start.7) | collective-permute-done | bytes 262176 | tf_op jit(solution)/shard_map/ppermute | solution.py:169
  154.6 1.0 shard_map.90
  (46 shorter events, 7.0 us)
Async XLA Ops:
  6.5 54.5 %all-to-all-start = ((bf16[32,4,64,128]{3,2,1,0:T(8,128)(2,1)}), bf16[32,4,64,128]{3,2,1,0:T(8,128)(2,1)S(1)}, u32[]{:S(2)}, u32[]{:S(2)}) async-start(bf16[32,4,64,128]{3,2,1,0:T(8,128)(2,1)} %bitcast.9), calls=%async_computation | async-start | bytes 4194304 | tf_op jit(solution)/shard_map/all_to_all | solution.py:190
  12.8 5.8 %copy-start.16 = (s32[2048]{0:T(1024)S(1)}, s32[2048]{0:T(1024)}, u32[]{:S(2)}) copy-start(s32[2048]{0:T(1024)} %param.5) | copy-start | bytes 24580
  61.0 1.3 copy-start
  62.3 56.4 %all-to-all-start.1 = ((bf16[32,4,64,128]{3,2,1,0:T(8,128)(2,1)}), bf16[32,4,64,128]{3,2,1,0:T(8,128)(2,1)S(1)}, u32[]{:S(2)}, u32[]{:S(2)}) async-start(bf16[32,4,64,128]{3,2,1,0:T(8,128)(2,1)} %bitcast.8), calls=%async_computation.1 | async-start | bytes 4194304 | tf_op jit(solution)/shard_map/all_to_all | solution.py:190
  66.2 1.6 %copy-start.1 = (bf16[32,4,64,128]{3,2,1,0:T(8,128)(2,1)S(1)}, bf16[32,4,64,128]{3,2,1,0:T(8,128)(2,1)}, u32[]{:S(2)}) copy-start(bf16[32,4,64,128]{3,2,1,0:T(8,128)(2,1)} %copy-done) | copy-start | bytes 6291460
  77.5 12.4 %collective-permute-start = (bf16[4,256,128]{2,1,0:T(8,128)(2,1)S(1)}, bf16[4,256,128]{2,1,0:T(8,128)(2,1)S(1)}, u32[]{:S(2)}, u32[]{:S(2)}) collective-permute-start(bf16[4,256,128]{2,1,0:T(8,128)(2,1)S(1)} %get-tuple-element.48), channel_id=1, source_target_pairs={{0,24},{4,28},{8,16},{12,20},{16,8},{20,12},{24,0},{28,4},{1,25},{... | collective-permute-start | bytes 786440 | tf_op jit(solution)/shard_map/ppermute | solution.py:169
  79.7 24.7 %collective-permute-start.1 = (bf16[4,256,128]{2,1,0:T(8,128)(2,1)S(1)}, bf16[4,256,128]{2,1,0:T(8,128)(2,1)S(1)}, u32[]{:S(2)}, u32[]{:S(2)}) collective-permute-start(bf16[4,256,128]{2,1,0:T(8,128)(2,1)S(1)} %get-tuple-element.49), channel_id=1, source_target_pairs={{0,28},{4,24},{8,20},{12,16},{16,12},{20,8},{24,4},{28,0},{1,29},{... | collective-permute-start | bytes 786440 | tf_op jit(solution)/shard_map/ppermute | solution.py:169
  80.5 29.7 %collective-permute-start.2 = (bf16[4,256,128]{2,1,0:T(8,128)(2,1)S(1)}, bf16[4,256,128]{2,1,0:T(8,128)(2,1)S(1)}, u32[]{:S(2)}, u32[]{:S(2)}) collective-permute-start(bf16[4,256,128]{2,1,0:T(8,128)(2,1)S(1)} %get-tuple-element.50), channel_id=1, source_target_pairs={{0,8},{4,12},{8,0},{12,4},{16,24},{20,28},{24,16},{28,20},{1,9},{5... | collective-permute-start | bytes 786440 | tf_op jit(solution)/shard_map/ppermute | solution.py:169
  81.7 29.2 %collective-permute-start.3 = (bf16[4,256,128]{2,1,0:T(8,128)(2,1)S(1)}, bf16[4,256,128]{2,1,0:T(8,128)(2,1)S(1)}, u32[]{:S(2)}, u32[]{:S(2)}) collective-permute-start(bf16[4,256,128]{2,1,0:T(8,128)(2,1)S(1)} %get-tuple-element.51), channel_id=1, source_target_pairs={{0,16},{4,20},{8,24},{12,28},{16,0},{20,4},{24,8},{28,12},{1,17},{... | collective-permute-start | bytes 786440 | tf_op jit(solution)/shard_map/ppermute | solution.py:169
  82.9 33.7 %collective-permute-start.4 = (bf16[4,256,128]{2,1,0:T(8,128)(2,1)S(1)}, bf16[4,256,128]{2,1,0:T(8,128)(2,1)S(1)}, u32[]{:S(2)}, u32[]{:S(2)}) collective-permute-start(bf16[4,256,128]{2,1,0:T(8,128)(2,1)S(1)} %get-tuple-element.52), channel_id=1, source_target_pairs={{0,12},{4,8},{8,4},{12,0},{16,28},{20,24},{24,20},{28,16},{1,13},{... | collective-permute-start | bytes 786440 | tf_op jit(solution)/shard_map/ppermute | solution.py:169
  89.9 0.7 copy-start.2
  90.6 26.7 %collective-permute-start.5 = (bf16[4,256,128]{2,1,0:T(8,128)(2,1)S(1)}, bf16[4,256,128]{2,1,0:T(8,128)(2,1)S(1)}, u32[]{:S(2)}, u32[]{:S(2)}) collective-permute-start(bf16[4,256,128]{2,1,0:T(8,128)(2,1)S(1)} %get-tuple-element.53), channel_id=1, source_target_pairs={{0,20},{4,16},{8,28},{12,24},{16,4},{20,0},{24,12},{28,8},{1,21},{... | collective-permute-start | bytes 786440 | tf_op jit(solution)/shard_map/ppermute | solution.py:169
  104.4 0.7 copy-start.4
  105.1 13.0 %collective-permute-start.6 = (bf16[4,256,128]{2,1,0:T(8,128)(2,1)S(1)}, bf16[4,256,128]{2,1,0:T(8,128)(2,1)S(1)}, u32[]{:S(2)}, u32[]{:S(2)}) collective-permute-start(bf16[4,256,128]{2,1,0:T(8,128)(2,1)S(1)} %get-tuple-element.54), channel_id=1, source_target_pairs={{0,4},{4,0},{8,12},{12,8},{16,20},{20,16},{24,28},{28,24},{1,5},{5... | collective-permute-start | bytes 786440 | tf_op jit(solution)/shard_map/ppermute | solution.py:169
  110.2 0.7 copy-start.6
  110.9 0.7 copy-start.8
  117.3 0.7 copy-start.12
  118.0 0.7 copy-start.14
  118.7 25.2 %copy-start.3 = (bf16[4,256,128]{2,1,0:T(8,128)(2,1)S(1)}, bf16[4,256,128]{2,1,0:T(8,128)(2,1)}, u32[]{:S(2)}) copy-start(bf16[4,256,128]{2,1,0:T(8,128)(2,1)} %copy-done.2) | copy-start | bytes 786436
  118.7 25.2 %copy-start.5 = (bf16[4,256,128]{2,1,0:T(8,128)(2,1)S(1)}, bf16[4,256,128]{2,1,0:T(8,128)(2,1)}, u32[]{:S(2)}) copy-start(bf16[4,256,128]{2,1,0:T(8,128)(2,1)} %copy-done.4) | copy-start | bytes 786436
  118.7 25.2 %copy-start.7 = (bf16[4,256,128]{2,1,0:T(8,128)(2,1)S(1)}, bf16[4,256,128]{2,1,0:T(8,128)(2,1)}, u32[]{:S(2)}) copy-start(bf16[4,256,128]{2,1,0:T(8,128)(2,1)} %copy-done.6) | copy-start | bytes 786436
  118.7 25.2 %copy-start.9 = (bf16[4,256,128]{2,1,0:T(8,128)(2,1)S(1)}, bf16[4,256,128]{2,1,0:T(8,128)(2,1)}, u32[]{:S(2)}) copy-start(bf16[4,256,128]{2,1,0:T(8,128)(2,1)} %copy-done.8) | copy-start | bytes 786436
  118.8 25.2 %copy-start.11 = (bf16[4,256,128]{2,1,0:T(8,128)(2,1)S(1)}, bf16[4,256,128]{2,1,0:T(8,128)(2,1)}, u32[]{:S(2)}) copy-start(bf16[4,256,128]{2,1,0:T(8,128)(2,1)} %copy-done.10) | copy-start | bytes 786436
  118.8 25.2 %copy-start.13 = (bf16[4,256,128]{2,1,0:T(8,128)(2,1)S(1)}, bf16[4,256,128]{2,1,0:T(8,128)(2,1)}, u32[]{:S(2)}) copy-start(bf16[4,256,128]{2,1,0:T(8,128)(2,1)} %copy-done.12) | copy-start | bytes 786436
  118.8 25.2 %copy-start.15 = (bf16[4,256,128]{2,1,0:T(8,128)(2,1)S(1)}, bf16[4,256,128]{2,1,0:T(8,128)(2,1)}, u32[]{:S(2)}) copy-start(bf16[4,256,128]{2,1,0:T(8,128)(2,1)} %copy-done.14) | copy-start | bytes 786436
  128.5 8.6 %collective-permute-start.10 = (bf16[4,256,128]{2,1,0:T(8,128)(2,1)S(1)}, bf16[4,256,128]{2,1,0:T(8,128)(2,1)S(1)}, u32[]{:S(2)}, u32[]{:S(2)}) collective-permute-start(bf16[4,256,128]{2,1,0:T(8,128)(2,1)S(1)} %get-tuple-element.60), channel_id=1, source_target_pairs={{0,24},{4,28},{8,16},{12,20},{16,8},{20,12},{24,0},{28,4},{1,25},{... | collective-permute-start | bytes 786440 | tf_op jit(solution)/shard_map/ppermute | solution.py:169
  130.5 13.4 %collective-permute-start.11 = (bf16[4,256,128]{2,1,0:T(8,128)(2,1)S(1)}, bf16[4,256,128]{2,1,0:T(8,128)(2,1)S(1)}, u32[]{:S(2)}, u32[]{:S(2)}) collective-permute-start(bf16[4,256,128]{2,1,0:T(8,128)(2,1)S(1)} %get-tuple-element.61), channel_id=1, source_target_pairs={{0,28},{4,24},{8,20},{12,16},{16,12},{20,8},{24,4},{28,0},{1,29},{... | collective-permute-start | bytes 786440 | tf_op jit(solution)/shard_map/ppermute | solution.py:169
  131.4 16.5 %collective-permute-start.12 = (bf16[4,256,128]{2,1,0:T(8,128)(2,1)S(1)}, bf16[4,256,128]{2,1,0:T(8,128)(2,1)S(1)}, u32[]{:S(2)}, u32[]{:S(2)}) collective-permute-start(bf16[4,256,128]{2,1,0:T(8,128)(2,1)S(1)} %get-tuple-element.62), channel_id=1, source_target_pairs={{0,8},{4,12},{8,0},{12,4},{16,24},{20,28},{24,16},{28,20},{1,9},{5... | collective-permute-start | bytes 786440 | tf_op jit(solution)/shard_map/ppermute | solution.py:169
  132.5 16.5 %collective-permute-start.13 = (bf16[4,256,128]{2,1,0:T(8,128)(2,1)S(1)}, bf16[4,256,128]{2,1,0:T(8,128)(2,1)S(1)}, u32[]{:S(2)}, u32[]{:S(2)}) collective-permute-start(bf16[4,256,128]{2,1,0:T(8,128)(2,1)S(1)} %get-tuple-element.63), channel_id=1, source_target_pairs={{0,16},{4,20},{8,24},{12,28},{16,0},{20,4},{24,8},{28,12},{1,17},{... | collective-permute-start | bytes 786440 | tf_op jit(solution)/shard_map/ppermute | solution.py:169
  133.4 20.7 %collective-permute-start.7 = (bf16[4,256,128]{2,1,0:T(8,128)(2,1)S(1)}, bf16[4,256,128]{2,1,0:T(8,128)(2,1)S(1)}, u32[]{:S(2)}, u32[]{:S(2)}) collective-permute-start(bf16[4,256,128]{2,1,0:T(8,128)(2,1)S(1)} %get-tuple-element.56), channel_id=1, source_target_pairs={{0,12},{4,8},{8,4},{12,0},{16,28},{20,24},{24,20},{28,16},{1,13},{... | collective-permute-start | bytes 786440 | tf_op jit(solution)/shard_map/ppermute | solution.py:169
  137.1 17.5 %collective-permute-start.8 = (bf16[4,256,128]{2,1,0:T(8,128)(2,1)S(1)}, bf16[4,256,128]{2,1,0:T(8,128)(2,1)S(1)}, u32[]{:S(2)}, u32[]{:S(2)}) collective-permute-start(bf16[4,256,128]{2,1,0:T(8,128)(2,1)S(1)} %get-tuple-element.57), channel_id=1, source_target_pairs={{0,20},{4,16},{8,28},{12,24},{16,4},{20,0},{24,12},{28,8},{1,21},{... | collective-permute-start | bytes 786440 | tf_op jit(solution)/shard_map/ppermute | solution.py:169
  143.9 10.7 %collective-permute-start.9 = (bf16[4,256,128]{2,1,0:T(8,128)(2,1)S(1)}, bf16[4,256,128]{2,1,0:T(8,128)(2,1)S(1)}, u32[]{:S(2)}, u32[]{:S(2)}) collective-permute-start(bf16[4,256,128]{2,1,0:T(8,128)(2,1)S(1)} %get-tuple-element.58), channel_id=1, source_target_pairs={{0,4},{4,0},{8,12},{12,8},{16,20},{20,16},{24,28},{28,24},{1,5},{5... | collective-permute-start | bytes 786440 | tf_op jit(solution)/shard_map/ppermute | solution.py:169
  (1 other events, 0.7 us)
where the time goes:
time: 158 us; the launch traced here: 156 us
  waiting for transfers between devices  82.7 us (52%)
  Pallas kernels  34.8 us (22%)
  starting transfers between devices  27.1 us (17%)
  local copies, waits for them, and re-layouts  8.33 us (5%)
  other arithmetic  1.82 us (1%)
    ppermute x14, waiting for transfers between devices, exchange(): lax.ppermute(value, 'seq', [(s, s ^ d) for s in range(lax.axis_size('seq'...  42.2 us
    all_to_all x2, waiting for transfers between devices, gather(): lax.all_to_all(parts, ('seq', 'chan'), split_axis=0, concat_axis=0, tiled...  40.4 us
    pallas_call x2, Pallas kernels, attention(): pl.pallas_call(functools.partial(attention_kernel, spans), out_shape=[low...  19.4 us
    ppermute x14, starting transfers between devices, exchange(): lax.ppermute(value, 'seq', [(s, s ^ d) for s in range(lax.axis_size('seq'...  17.2 us
    pallas_call x2, Pallas kernels, pack(): pl.pallas_call(functools.partial(pack_kernel, owners), grid=(chans, 2), o...  11.7 us
    all_to_all x2, starting transfers between devices, gather(): lax.all_to_all(parts, ('seq', 'chan'), split_axis=0, concat_axis=0, tiled...  9.87 us
    unnamed x34, local copies, waits for them, and re-layouts  7.87 us
    pallas_call x3, Pallas kernels, unpack(): pl.pallas_call(functools.partial(unpack_kernel, peers, base), out_shape=[...  3.75 us
  transfers between devices with their start and end apart: 16, of which 11 were waited for; matrix products, arithmetic and copies ran while one was open for 1% of the time, Pallas kernels for 12%

commit v1 on v0

--- a/solution.py
+++ b/solution.py
@@ -38,25 +38,31 @@
     return lax.dot_general(a, b, (((0,), (0,)), ((), ())), preferred_element_type=jnp.float32)
 
 
-def pack_kernel(owners, *refs):
-    ins, out_ref = refs[:4], refs[4]
-    for owner in range(owners):
-        for which in range(4):
-            out_ref[owner, 0, which] = ins[which][:, owner * HEAD_DIM : (owner + 1) * HEAD_DIM]
+def pack_kernel(owners, chans, *refs):
+    ins, out_ref = refs[:-1], refs[-1]
+    for chan in range(chans):
+        for owner in range(owners):
+            for which in range(4):
+                columns = slice(owner * HEAD_DIM, (owner + 1) * HEAD_DIM)
+                out_ref[owner, chan, which] = ins[4 * chan + which][:, columns]
 
 
 def pack(inputs, chans, turns, turn):
     rows, width = inputs[0].shape
     owners = width // HEAD_DIM // chans // turns
+
+    def columns(chan):
+        return pl.BlockSpec((rows, owners * HEAD_DIM), lambda i: (0, chan * turns + turn))
+
     return pl.pallas_call(
-        functools.partial(pack_kernel, owners),
-        grid=(chans, 2),
+        functools.partial(pack_kernel, owners, chans),
+        grid=(1,),
         out_shape=low_array(owners, chans, 4, rows, HEAD_DIM),
-        in_specs=[pl.BlockSpec((rows // 2, owners * HEAD_DIM), lambda c, r: (r, c * turns + turn))]
-        * 4,
-        out_specs=pl.BlockSpec((owners, 1, 4, rows // 2, HEAD_DIM), lambda c, r: (0, c, 0, r, 0)),
+        in_specs=[columns(chan) for chan in range(chans) for _ in range(4)],
+        out_specs=pl.BlockSpec((owners, chans, 4, rows, HEAD_DIM), lambda i: (0, 0, 0, 0, 0)),
+        compiler_params=pltpu.CompilerParams(vmem_limit_bytes=20 << 20),
         cost_estimate=moved(16 * rows * width // turns),
-    )(*inputs)
+    )(*(list(inputs) * chans))
 
 
 def attention_kernel(spans, count_ref, start_ref, target_ref, in_ref, *refs):
@@ -197,9 +203,7 @@
     outs, blocks = (), ()
     for turn in range(turns):
         following = gather(parts[turn]) if turn + 1 < turns else None
-        mine, blocks = tied((mine, blocks))
-        if turn > 0:
-            outs = unpack(place, blocks, order, (turn - 1) * owners, heads * HEAD_DIM, outs)
+        mine, outs = tied((mine, outs))
         blocks = list(attention(count, start, peers, mine))
         if copies == 1:
             blocks = [exchange(blocks[d], d) if d else blocks[d] for d in order]
@@ -209,10 +213,11 @@
             whole = lax.all_to_all(whole, "seq", split_axis=0, concat_axis=0, tiled=True)
             blocks = [whole[owner * copies] for owner in range(owners)]
             place, order = jnp.zeros((1,), jnp.int32), list(range(owners))
+        early, base = len(blocks) // 2 + 1, turn * owners
+        outs = unpack(place, blocks[:early], order[:early], base, heads * HEAD_DIM, outs)
+        outs = unpack(place, blocks[early:], order[early:], base, heads * HEAD_DIM, outs)
         mine = following
-    early, base = len(blocks) // 2 + 1, (turns - 1) * owners
-    outs = unpack(place, blocks[:early], order[:early], base, heads * HEAD_DIM, outs)
-    return tuple(unpack(place, blocks[early:], order[early:], base, heads * HEAD_DIM, outs))
+    return tuple(outs)
 
 
 def solution(mesh):

time: 158 us -> 157 us (level)
  Pallas kernels: 34.8 us -> 26.7 us
  waiting for transfers between devices: 82.7 us -> 88.9 us
    pallas_call x2, Pallas kernels: 11.7 us -> 0.99 us  [pack(): pl.pallas_call(functools.partial(pack_kernel, owners, chans), grid=(1,),...]
    ppermute x14, waiting for transfers between devices: 42.2 us -> 45.7 us  [exchange(): lax.ppermute(value, 'seq', [(s, s ^ d) for s in range(lax.axis_size('seq'...]
    all_to_all x2, waiting for transfers between devices: 40.4 us -> 43.2 us  [gather(): lax.all_to_all(parts, ('seq', 'chan'), split_axis=0, concat_axis=0, tiled...]
    pallas_call x2, Pallas kernels: 19.4 us -> 21.4 us  [attention(): pl.pallas_call(functools.partial(attention_kernel, spans), out_shape=[low...]
    unnamed x34 -> x22, local copies, waits for them, and re-layouts: 7.87 us -> 8.8 us
    pallas_call x3 -> x4, Pallas kernels: 3.75 us -> 4.36 us  [unpack(): pl.pallas_call(functools.partial(unpack_kernel, peers, base), out_shape=[...]
  transfers between devices with their start and end apart: 16 -> 16, of which waited for: 11 -> 10; matrix products, arithmetic and copies ran while one was open for 1% -> 1% of each run, Pallas kernels for 12% -> 10%
where the time goes in v1:
time: 157 us; the launch traced here: 156 us
  waiting for transfers between devices  88.9 us (57%)
  starting transfers between devices  28.2 us (18%)
  Pallas kernels  26.7 us (17%)
  local copies, waits for them, and re-layouts  9.25 us (6%)
  other arithmetic  1.81 us (1%)
    ppermute x14, waiting for transfers between devices, exchange(): lax.ppermute(value, 'seq', [(s, s ^ d) for s in range(lax.axis_size('seq'...  45.7 us
    all_to_all x2, waiting for transfers between devices, gather(): lax.all_to_all(parts, ('seq', 'chan'), split_axis=0, concat_axis=0, tiled...  43.2 us
    pallas_call x2, Pallas kernels, attention(): pl.pallas_call(functools.partial(attention_kernel, spans), out_shape=[low...  21.4 us
    ppermute x14, starting transfers between devices, exchange(): lax.ppermute(value, 'seq', [(s, s ^ d) for s in range(lax.axis_size('seq'...  18.3 us
    all_to_all x2, starting transfers between devices, gather(): lax.all_to_all(parts, ('seq', 'chan'), split_axis=0, concat_axis=0, tiled...  9.92 us
    unnamed x22, local copies, waits for them, and re-layouts  8.8 us
    pallas_call x4, Pallas kernels, unpack(): pl.pallas_call(functools.partial(unpack_kernel, peers, base), out_shape=[...  4.36 us
  transfers between devices with their start and end apart: 16, of which 10 were waited for; matrix products, arithmetic and copies ran while one was open for 1% of the time, Pallas kernels for 10%

profile of v1, /device:TPU:9, one launch (start us, length us, event | category | flops | bytes accessed | tf_op | source)
XLA Modules:
  0.0 155.9 jit_solution(10907720753195606264)
XLA Ops:
  0.6 1.2 copy-done
  1.9 1.2 copy-done.2
  3.1 1.2 copy-done.4
  4.3 1.2 copy-done.6
  6.0 1.4 copy-done.9
  7.4 6.4 %all-to-all-start = ((bf16[32,4,64,128]{3,2,1,0:T(8,128)(2,1)}), bf16[32,4,64,128]{3,2,1,0:T(8,128)(2,1)}, u32[]{:S(2)}, u32[]{:S(2)}) async-start(bf16[32,4,64,128]{3,2,1,0:T(8,128)(2,1)} %bitcast.7), calls=%async_computation | async-start | bytes 4194304 | tf_op jit(solution)/shard_map/all_to_all | solution.py:196
  13.9 1.2 copy-done.7
  15.6 1.3 copy-done.8
  16.9 1.8 %convert_reduce_fusion = s32[2048]{0:T(1024)S(1)} fusion(s32[2048]{0:T(1024)S(1)} %copy-done.10), kind=kLoop, calls=%fused_computation | loop fusion | flops 12580864 | bytes 16384 | tf_op jit(solution)/shard_map/reduce_sum | solution.py:187
  18.8 43.2 %all-to-all-done = bf16[32,4,64,128]{3,2,1,0:T(8,128)(2,1)} async-done(((bf16[32,4,64,128]{3,2,1,0:T(8,128)(2,1)}), bf16[32,4,64,128]{3,2,1,0:T(8,128)(2,1)}, u32[]{:S(2)}, u32[]{:S(2)}) %all-to-all-start) | async-done | bytes 2097184 | tf_op jit(solution)/shard_map/all_to_all | solution.py:196
  62.0 3.5 %all-to-all-start.1 = ((bf16[32,4,64,128]{3,2,1,0:T(8,128)(2,1)}), bf16[32,4,64,128]{3,2,1,0:T(8,128)(2,1)S(1)}, u32[]{:S(2)}, u32[]{:S(2)}) async-start(bf16[32,4,64,128]{3,2,1,0:T(8,128)(2,1)} %bitcast.6), calls=%async_computation.1 | async-start | bytes 4194304 | tf_op jit(solution)/shard_map/all_to_all | solution.py:196
  66.0 11.2 %shard_map.86 = (bf16[4,256,128]{2,1,0:T(8,128)(2,1)S(1)}, bf16[4,256,128]{2,1,0:T(8,128)(2,1)S(1)}, bf16[4,256,128]{2,1,0:T(8,128)(2,1)S(1)}, bf16[4,256,128]{2...) custom-call(s32[8]{0:T(128)S(1)} %subtract_add_fusion.count_ref, ...), custom_call_target="tpu_custom_call" | custom-call | flops 2415919104 | bytes 4194304 | tf_op jit(solution)/shard_map/pallas_call | solution.py:124
  77.2 2.2 %collective-permute-start.3 = (bf16[4,256,128]{2,1,0:T(8,128)(2,1)S(1)}, bf16[4,256,128]{2,1,0:T(8,128)(2,1)S(1)}, u32[]{:S(2)}, u32[]{:S(2)}) collective-permute-start(bf16[4,256,128]{2,1,0:T(8,128)(2,1)S(1)} %get-tuple-element.51), channel_id=1, source_target_pairs={{0,24},{4,28},{8,16},{12,20},{16,8},{20,12},{24,0},{28,4},{1,25},{... | collective-permute-start | bytes 786440 | tf_op jit(solution)/shard_map/ppermute | solution.py:175
  81.4 1.2 collective-permute-start.6
  82.6 7.1 %collective-permute-done.3.refs_1_ = bf16[4,256,128]{2,1,0:T(8,128)(2,1)S(1)} collective-permute-done((bf16[4,256,128]{2,1,0:T(8,128)(2,1)S(1)}, bf16[4,256,128]{2,1,0:T(8,128)(2,1)S(1)}, u32[]{:S(2)}, u32[]{:S(2)}) %collective-permute-start.3) | collective-permute-done | bytes 262176 | tf_op jit(solution)/shard_map/ppermute | solution.py:175
  89.6 3.8 %collective-permute-start.1 = (bf16[4,256,128]{2,1,0:T(8,128)(2,1)S(1)}, bf16[4,256,128]{2,1,0:T(8,128)(2,1)S(1)}, u32[]{:S(2)}, u32[]{:S(2)}) collective-permute-start(bf16[4,256,128]{2,1,0:T(8,128)(2,1)S(1)} %get-tuple-element.48), channel_id=1, source_target_pairs={{0,20},{4,16},{8,28},{12,24},{16,4},{20,0},{24,12},{28,8},{1,21},{... | collective-permute-start | bytes 786440 | tf_op jit(solution)/shard_map/ppermute | solution.py:175
  93.4 10.6 %collective-permute-done.4.refs_2_ = bf16[4,256,128]{2,1,0:T(8,128)(2,1)S(1)} collective-permute-done((bf16[4,256,128]{2,1,0:T(8,128)(2,1)S(1)}, bf16[4,256,128]{2,1,0:T(8,128)(2,1)S(1)}, u32[]{:S(2)}, u32[]{:S(2)}) %collective-permute-start.4) | collective-permute-done | bytes 262176 | tf_op jit(solution)/shard_map/ppermute | solution.py:175
  104.1 12.1 %collective-permute-done.5.refs_3_ = bf16[4,256,128]{2,1,0:T(8,128)(2,1)S(1)} collective-permute-done((bf16[4,256,128]{2,1,0:T(8,128)(2,1)S(1)}, bf16[4,256,128]{2,1,0:T(8,128)(2,1)S(1)}, u32[]{:S(2)}, u32[]{:S(2)}) %collective-permute-start.5) | collective-permute-done | bytes 262176 | tf_op jit(solution)/shard_map/ppermute | solution.py:175
  116.2 1.2 shard_map.87
  117.5 1.0 shard_map.88
  118.5 10.2 %shard_map.89 = (bf16[4,256,128]{2,1,0:T(8,128)(2,1)S(1)}, bf16[4,256,128]{2,1,0:T(8,128)(2,1)S(1)}, bf16[4,256,128]{2,1,0:T(8,128)(2,1)S(1)}, bf16[4,256,128]{2...) custom-call(s32[8]{0:T(128)S(1)} %subtract_add_fusion.count_ref, ...), custom_call_target="tpu_custom_call" | custom-call | flops 2415919104 | bytes 4194304 | tf_op jit(solution)/shard_map/pallas_call | solution.py:124
  128.6 1.7 %collective-permute-start.10 = (bf16[4,256,128]{2,1,0:T(8,128)(2,1)S(1)}, bf16[4,256,128]{2,1,0:T(8,128)(2,1)S(1)}, u32[]{:S(2)}, u32[]{:S(2)}) collective-permute-start(bf16[4,256,128]{2,1,0:T(8,128)(2,1)S(1)} %get-tuple-element.68), channel_id=1, source_target_pairs={{0,24},{4,28},{8,16},{12,20},{16,8},{20,12},{24,0},{28,4},{1,25},{... | collective-permute-start | bytes 786440 | tf_op jit(solution)/shard_map/ppermute | solution.py:175
  130.3 1.7 %collective-permute-start.11 = (bf16[4,256,128]{2,1,0:T(8,128)(2,1)S(1)}, bf16[4,256,128]{2,1,0:T(8,128)(2,1)S(1)}, u32[]{:S(2)}, u32[]{:S(2)}) collective-permute-start(bf16[4,256,128]{2,1,0:T(8,128)(2,1)S(1)} %get-tuple-element.69), channel_id=1, source_target_pairs={{0,28},{4,24},{8,20},{12,16},{16,12},{20,8},{24,4},{28,0},{1,29},{... | collective-permute-start | bytes 786440 | tf_op jit(solution)/shard_map/ppermute | solution.py:175
  132.0 1.0 collective-permute-start.12
  133.0 1.2 collective-permute-start.13
  134.2 2.5 %collective-permute-done.10.refs_1_ = bf16[4,256,128]{2,1,0:T(8,128)(2,1)S(1)} collective-permute-done((bf16[4,256,128]{2,1,0:T(8,128)(2,1)S(1)}, bf16[4,256,128]{2,1,0:T(8,128)(2,1)S(1)}, u32[]{:S(2)}, u32[]{:S(2)}) %collective-permute-start.10) | collective-permute-done | bytes 262176 | tf_op jit(solution)/shard_map/ppermute | solution.py:175
  136.7 3.5 %collective-permute-start.8 = (bf16[4,256,128]{2,1,0:T(8,128)(2,1)S(1)}, bf16[4,256,128]{2,1,0:T(8,128)(2,1)S(1)}, u32[]{:S(2)}, u32[]{:S(2)}) collective-permute-start(bf16[4,256,128]{2,1,0:T(8,128)(2,1)S(1)} %get-tuple-element.65), channel_id=1, source_target_pairs={{0,20},{4,16},{8,28},{12,24},{16,4},{20,0},{24,12},{28,8},{1,21},{... | collective-permute-start | bytes 786440 | tf_op jit(solution)/shard_map/ppermute | solution.py:175
  140.2 4.4 %collective-permute-done.11.refs_2_ = bf16[4,256,128]{2,1,0:T(8,128)(2,1)S(1)} collective-permute-done((bf16[4,256,128]{2,1,0:T(8,128)(2,1)S(1)}, bf16[4,256,128]{2,1,0:T(8,128)(2,1)S(1)}, u32[]{:S(2)}, u32[]{:S(2)}) %collective-permute-start.11) | collective-permute-done | bytes 262176 | tf_op jit(solution)/shard_map/ppermute | solution.py:175
  144.6 2.2 %collective-permute-done.12.refs_3_ = bf16[4,256,128]{2,1,0:T(8,128)(2,1)S(1)} collective-permute-done((bf16[4,256,128]{2,1,0:T(8,128)(2,1)S(1)}, bf16[4,256,128]{2,1,0:T(8,128)(2,1)S(1)}, u32[]{:S(2)}, u32[]{:S(2)}) %collective-permute-start.12) | collective-permute-done | bytes 262176 | tf_op jit(solution)/shard_map/ppermute | solution.py:175
  146.7 2.4 %collective-permute-done.13.refs_4_ = bf16[4,256,128]{2,1,0:T(8,128)(2,1)S(1)} collective-permute-done((bf16[4,256,128]{2,1,0:T(8,128)(2,1)S(1)}, bf16[4,256,128]{2,1,0:T(8,128)(2,1)S(1)}, u32[]{:S(2)}, u32[]{:S(2)}) %collective-permute-start.13) | collective-permute-done | bytes 262176 | tf_op jit(solution)/shard_map/ppermute | solution.py:175
  149.1 1.2 shard_map.90
  150.4 3.6 %collective-permute-done.7.refs_0_ = bf16[4,256,128]{2,1,0:T(8,128)(2,1)S(1)} collective-permute-done((bf16[4,256,128]{2,1,0:T(8,128)(2,1)S(1)}, bf16[4,256,128]{2,1,0:T(8,128)(2,1)S(1)}, u32[]{:S(2)}, u32[]{:S(2)}) %collective-permute-start.7) | collective-permute-done | bytes 262176 | tf_op jit(solution)/shard_map/ppermute | solution.py:175
  (35 shorter events, 5.4 us)
Async XLA Ops:
  0.6 1.2 copy-start
  1.9 1.2 copy-start.2
  3.1 1.2 copy-start.4
  4.3 1.2 copy-start.6
  6.0 1.4 copy-start.9
  7.4 6.4 %copy-start.1 = (bf16[64,8192]{1,0:T(8,128)(2,1)S(1)}, bf16[64,8192]{1,0:T(8,128)(2,1)}, u32[]{:S(2)}) copy-start(bf16[64,8192]{1,0:T(8,128)(2,1)} %refs_12_.3) | copy-start | bytes 3145732
  7.4 6.4 %copy-start.3 = (bf16[64,8192]{1,0:T(8,128)(2,1)S(1)}, bf16[64,8192]{1,0:T(8,128)(2,1)}, u32[]{:S(2)}) copy-start(bf16[64,8192]{1,0:T(8,128)(2,1)} %refs_13_.3) | copy-start | bytes 3145732
  7.4 6.4 %copy-start.5 = (bf16[64,8192]{1,0:T(8,128)(2,1)S(1)}, bf16[64,8192]{1,0:T(8,128)(2,1)}, u32[]{:S(2)}) copy-start(bf16[64,8192]{1,0:T(8,128)(2,1)} %refs_14_.3) | copy-start | bytes 3145732
  7.4 54.6 %all-to-all-start = ((bf16[32,4,64,128]{3,2,1,0:T(8,128)(2,1)}), bf16[32,4,64,128]{3,2,1,0:T(8,128)(2,1)}, u32[]{:S(2)}, u32[]{:S(2)}) async-start(bf16[32,4,64,128]{3,2,1,0:T(8,128)(2,1)} %bitcast.7), calls=%async_computation | async-start | bytes 4194304 | tf_op jit(solution)/shard_map/all_to_all | solution.py:196
  13.9 1.2 copy-start.7
  15.1 1.8 %copy-start.10 = (s32[2048]{0:T(1024)S(1)}, s32[2048]{0:T(1024)}, u32[]{:S(2)}) copy-start(s32[2048]{0:T(1024)} %param.5) | copy-start | bytes 24580
  15.6 1.3 copy-start.8
  62.0 56.4 %all-to-all-start.1 = ((bf16[32,4,64,128]{3,2,1,0:T(8,128)(2,1)}), bf16[32,4,64,128]{3,2,1,0:T(8,128)(2,1)S(1)}, u32[]{:S(2)}, u32[]{:S(2)}) async-start(bf16[32,4,64,128]{3,2,1,0:T(8,128)(2,1)} %bitcast.6), calls=%async_computation.1 | async-start | bytes 4194304 | tf_op jit(solution)/shard_map/all_to_all | solution.py:196
  77.2 12.5 %collective-permute-start.3 = (bf16[4,256,128]{2,1,0:T(8,128)(2,1)S(1)}, bf16[4,256,128]{2,1,0:T(8,128)(2,1)S(1)}, u32[]{:S(2)}, u32[]{:S(2)}) collective-permute-start(bf16[4,256,128]{2,1,0:T(8,128)(2,1)S(1)} %get-tuple-element.51), channel_id=1, source_target_pairs={{0,24},{4,28},{8,16},{12,20},{16,8},{20,12},{24,0},{28,4},{1,25},{... | collective-permute-start | bytes 786440 | tf_op jit(solution)/shard_map/ppermute | solution.py:175
  79.3 24.8 %collective-permute-start.4 = (bf16[4,256,128]{2,1,0:T(8,128)(2,1)S(1)}, bf16[4,256,128]{2,1,0:T(8,128)(2,1)S(1)}, u32[]{:S(2)}, u32[]{:S(2)}) collective-permute-start(bf16[4,256,128]{2,1,0:T(8,128)(2,1)S(1)} %get-tuple-element.52), channel_id=1, source_target_pairs={{0,28},{4,24},{8,20},{12,16},{16,12},{20,8},{24,4},{28,0},{1,29},{... | collective-permute-start | bytes 786440 | tf_op jit(solution)/shard_map/ppermute | solution.py:175
  80.1 37.3 %collective-permute-start = (bf16[4,256,128]{2,1,0:T(8,128)(2,1)S(1)}, bf16[4,256,128]{2,1,0:T(8,128)(2,1)S(1)}, u32[]{:S(2)}, u32[]{:S(2)}) collective-permute-start(bf16[4,256,128]{2,1,0:T(8,128)(2,1)S(1)} %get-tuple-element.47), channel_id=1, source_target_pairs={{0,12},{4,8},{8,4},{12,0},{16,28},{20,24},{24,20},{28,16},{1,13},{... | collective-permute-start | bytes 786440 | tf_op jit(solution)/shard_map/ppermute | solution.py:175
  81.1 35.1 %collective-permute-start.5 = (bf16[4,256,128]{2,1,0:T(8,128)(2,1)S(1)}, bf16[4,256,128]{2,1,0:T(8,128)(2,1)S(1)}, u32[]{:S(2)}, u32[]{:S(2)}) collective-permute-start(bf16[4,256,128]{2,1,0:T(8,128)(2,1)S(1)} %get-tuple-element.53), channel_id=1, source_target_pairs={{0,8},{4,12},{8,0},{12,4},{16,24},{20,28},{24,16},{28,20},{1,9},{5... | collective-permute-start | bytes 786440 | tf_op jit(solution)/shard_map/ppermute | solution.py:175
  81.4 34.9 %collective-permute-start.6 = (bf16[4,256,128]{2,1,0:T(8,128)(2,1)S(1)}, bf16[4,256,128]{2,1,0:T(8,128)(2,1)S(1)}, u32[]{:S(2)}, u32[]{:S(2)}) collective-permute-start(bf16[4,256,128]{2,1,0:T(8,128)(2,1)S(1)} %get-tuple-element.54), channel_id=1, source_target_pairs={{0,16},{4,20},{8,24},{12,28},{16,0},{20,4},{24,8},{28,12},{1,17},{... | collective-permute-start | bytes 786440 | tf_op jit(solution)/shard_map/ppermute | solution.py:175
  89.6 27.8 %collective-permute-start.1 = (bf16[4,256,128]{2,1,0:T(8,128)(2,1)S(1)}, bf16[4,256,128]{2,1,0:T(8,128)(2,1)S(1)}, u32[]{:S(2)}, u32[]{:S(2)}) collective-permute-start(bf16[4,256,128]{2,1,0:T(8,128)(2,1)S(1)} %get-tuple-element.48), channel_id=1, source_target_pairs={{0,20},{4,16},{8,28},{12,24},{16,4},{20,0},{24,12},{28,8},{1,21},{... | collective-permute-start | bytes 786440 | tf_op jit(solution)/shard_map/ppermute | solution.py:175
  104.1 13.4 %collective-permute-start.2 = (bf16[4,256,128]{2,1,0:T(8,128)(2,1)S(1)}, bf16[4,256,128]{2,1,0:T(8,128)(2,1)S(1)}, u32[]{:S(2)}, u32[]{:S(2)}) collective-permute-start(bf16[4,256,128]{2,1,0:T(8,128)(2,1)S(1)} %get-tuple-element.49), channel_id=1, source_target_pairs={{0,4},{4,0},{8,12},{12,8},{16,20},{20,16},{24,28},{28,24},{1,5},{5... | collective-permute-start | bytes 786440 | tf_op jit(solution)/shard_map/ppermute | solution.py:175
  128.6 8.0 %collective-permute-start.10 = (bf16[4,256,128]{2,1,0:T(8,128)(2,1)S(1)}, bf16[4,256,128]{2,1,0:T(8,128)(2,1)S(1)}, u32[]{:S(2)}, u32[]{:S(2)}) collective-permute-start(bf16[4,256,128]{2,1,0:T(8,128)(2,1)S(1)} %get-tuple-element.68), channel_id=1, source_target_pairs={{0,24},{4,28},{8,16},{12,20},{16,8},{20,12},{24,0},{28,4},{1,25},{... | collective-permute-start | bytes 786440 | tf_op jit(solution)/shard_map/ppermute | solution.py:175
  130.3 14.3 %collective-permute-start.11 = (bf16[4,256,128]{2,1,0:T(8,128)(2,1)S(1)}, bf16[4,256,128]{2,1,0:T(8,128)(2,1)S(1)}, u32[]{:S(2)}, u32[]{:S(2)}) collective-permute-start(bf16[4,256,128]{2,1,0:T(8,128)(2,1)S(1)} %get-tuple-element.69), channel_id=1, source_target_pairs={{0,28},{4,24},{8,20},{12,16},{16,12},{20,8},{24,4},{28,0},{1,29},{... | collective-permute-start | bytes 786440 | tf_op jit(solution)/shard_map/ppermute | solution.py:175
  132.0 14.7 %collective-permute-start.12 = (bf16[4,256,128]{2,1,0:T(8,128)(2,1)S(1)}, bf16[4,256,128]{2,1,0:T(8,128)(2,1)S(1)}, u32[]{:S(2)}, u32[]{:S(2)}) collective-permute-start(bf16[4,256,128]{2,1,0:T(8,128)(2,1)S(1)} %get-tuple-element.70), channel_id=1, source_target_pairs={{0,8},{4,12},{8,0},{12,4},{16,24},{20,28},{24,16},{28,20},{1,9},{5... | collective-permute-start | bytes 786440 | tf_op jit(solution)/shard_map/ppermute | solution.py:175
  133.0 16.1 %collective-permute-start.13 = (bf16[4,256,128]{2,1,0:T(8,128)(2,1)S(1)}, bf16[4,256,128]{2,1,0:T(8,128)(2,1)S(1)}, u32[]{:S(2)}, u32[]{:S(2)}) collective-permute-start(bf16[4,256,128]{2,1,0:T(8,128)(2,1)S(1)} %get-tuple-element.71), channel_id=1, source_target_pairs={{0,16},{4,20},{8,24},{12,28},{16,0},{20,4},{24,8},{28,12},{1,17},{... | collective-permute-start | bytes 786440 | tf_op jit(solution)/shard_map/ppermute | solution.py:175
  134.2 19.7 %collective-permute-start.7 = (bf16[4,256,128]{2,1,0:T(8,128)(2,1)S(1)}, bf16[4,256,128]{2,1,0:T(8,128)(2,1)S(1)}, u32[]{:S(2)}, u32[]{:S(2)}) collective-permute-start(bf16[4,256,128]{2,1,0:T(8,128)(2,1)S(1)} %get-tuple-element.64), channel_id=1, source_target_pairs={{0,12},{4,8},{8,4},{12,0},{16,28},{20,24},{24,20},{28,16},{1,13},{... | collective-permute-start | bytes 786440 | tf_op jit(solution)/shard_map/ppermute | solution.py:175
  136.7 18.1 %collective-permute-start.8 = (bf16[4,256,128]{2,1,0:T(8,128)(2,1)S(1)}, bf16[4,256,128]{2,1,0:T(8,128)(2,1)S(1)}, u32[]{:S(2)}, u32[]{:S(2)}) collective-permute-start(bf16[4,256,128]{2,1,0:T(8,128)(2,1)S(1)} %get-tuple-element.65), channel_id=1, source_target_pairs={{0,20},{4,16},{8,28},{12,24},{16,4},{20,0},{24,12},{28,8},{1,21},{... | collective-permute-start | bytes 786440 | tf_op jit(solution)/shard_map/ppermute | solution.py:175
  144.6 10.2 %collective-permute-start.9 = (bf16[4,256,128]{2,1,0:T(8,128)(2,1)S(1)}, bf16[4,256,128]{2,1,0:T(8,128)(2,1)S(1)}, u32[]{:S(2)}, u32[]{:S(2)}) collective-permute-start(bf16[4,256,128]{2,1,0:T(8,128)(2,1)S(1)} %get-tuple-element.66), channel_id=1, source_target_pairs={{0,4},{4,0},{8,12},{12,8},{16,20},{20,16},{24,28},{28,24},{1,5},{5... | collective-permute-start | bytes 786440 | tf_op jit(solution)/shard_map/ppermute | solution.py:175

commit v2 on v0

--- a/solution.py
+++ b/solution.py
@@ -50,11 +50,10 @@
     owners = width // HEAD_DIM // chans // turns
     return pl.pallas_call(
         functools.partial(pack_kernel, owners),
-        grid=(chans, 2),
+        grid=(chans,),
         out_shape=low_array(owners, chans, 4, rows, HEAD_DIM),
-        in_specs=[pl.BlockSpec((rows // 2, owners * HEAD_DIM), lambda c, r: (r, c * turns + turn))]
-        * 4,
-        out_specs=pl.BlockSpec((owners, 1, 4, rows // 2, HEAD_DIM), lambda c, r: (0, c, 0, r, 0)),
+        in_specs=[pl.BlockSpec((rows, owners * HEAD_DIM), lambda c: (0, c * turns + turn))] * 4,
+        out_specs=pl.BlockSpec((owners, 1, 4, rows, HEAD_DIM), lambda c: (0, c, 0, 0, 0)),
         cost_estimate=moved(16 * rows * width // turns),
     )(*inputs)
 
@@ -197,9 +196,7 @@
     outs, blocks = (), ()
     for turn in range(turns):
         following = gather(parts[turn]) if turn + 1 < turns else None
-        mine, blocks = tied((mine, blocks))
-        if turn > 0:
-            outs = unpack(place, blocks, order, (turn - 1) * owners, heads * HEAD_DIM, outs)
+        mine, outs = tied((mine, outs))
         blocks = list(attention(count, start, peers, mine))
         if copies == 1:
             blocks = [exchange(blocks[d], d) if d else blocks[d] for d in order]
@@ -209,10 +206,11 @@
             whole = lax.all_to_all(whole, "seq", split_axis=0, concat_axis=0, tiled=True)
             blocks = [whole[owner * copies] for owner in range(owners)]
             place, order = jnp.zeros((1,), jnp.int32), list(range(owners))
+        early, base = len(blocks) // 2 + 1, turn * owners
+        outs = unpack(place, blocks[:early], order[:early], base, heads * HEAD_DIM, outs)
+        outs = unpack(place, blocks[early:], order[early:], base, heads * HEAD_DIM, outs)
         mine = following
-    early, base = len(blocks) // 2 + 1, (turns - 1) * owners
-    outs = unpack(place, blocks[:early], order[:early], base, heads * HEAD_DIM, outs)
-    return tuple(unpack(place, blocks[early:], order[early:], base, heads * HEAD_DIM, outs))
+    return tuple(outs)
 
 
 def solution(mesh):

time: 158 us -> 155 us (0.981)
  waiting for transfers between devices: 82.7 us -> 88 us
  local copies, waits for them, and re-layouts: 8.33 us -> 3.34 us
  Pallas kernels: 34.8 us -> 32.3 us
    unnamed x34 -> x6, local copies, waits for them, and re-layouts: 7.87 us -> 2.89 us
    pallas_call x2, Pallas kernels: 11.7 us -> 7.96 us  [pack(): pl.pallas_call(functools.partial(pack_kernel, owners), grid=(chans,), out...]
    ppermute x14, waiting for transfers between devices: 42.2 us -> 45.8 us  [exchange(): lax.ppermute(value, 'seq', [(s, s ^ d) for s in range(lax.axis_size('seq'...]
    all_to_all x2, waiting for transfers between devices: 40.4 us -> 42.2 us  [gather(): lax.all_to_all(parts, ('seq', 'chan'), split_axis=0, concat_axis=0, tiled...]
    pallas_call x3 -> x4, Pallas kernels: 3.75 us -> 4.36 us  [unpack(): pl.pallas_call(functools.partial(unpack_kernel, peers, base), out_shape=[...]
  transfers between devices with their start and end apart: 16 -> 16, of which waited for: 11 -> 10; matrix products, arithmetic and copies ran while one was open for 1% -> 1% of each run, Pallas kernels for 12% -> 11%
where the time goes in v2:
time: 155 us; the launch traced here: 154 us
  waiting for transfers between devices  88 us (57%)
  Pallas kernels  32.3 us (21%)
  starting transfers between devices  27.8 us (18%)
  local copies, waits for them, and re-layouts  3.34 us (2%)
  other arithmetic  1.82 us (1%)
    ppermute x14, waiting for transfers between devices, exchange(): lax.ppermute(value, 'seq', [(s, s ^ d) for s in range(lax.axis_size('seq'...  45.8 us
    all_to_all x2, waiting for transfers between devices, gather(): lax.all_to_all(parts, ('seq', 'chan'), split_axis=0, concat_axis=0, tiled...  42.2 us
    pallas_call x2, Pallas kernels, attention(): pl.pallas_call(functools.partial(attention_kernel, spans), out_shape=[low...  20 us
    ppermute x14, starting transfers between devices, exchange(): lax.ppermute(value, 'seq', [(s, s ^ d) for s in range(lax.axis_size('seq'...  18 us
    all_to_all x2, starting transfers between devices, gather(): lax.all_to_all(parts, ('seq', 'chan'), split_axis=0, concat_axis=0, tiled...  9.87 us
    pallas_call x2, Pallas kernels, pack(): pl.pallas_call(functools.partial(pack_kernel, owners), grid=(chans,), out...  7.96 us
    pallas_call x4, Pallas kernels, unpack(): pl.pallas_call(functools.partial(unpack_kernel, peers, base), out_shape=[...  4.36 us
  transfers between devices with their start and end apart: 16, of which 10 were waited for; matrix products, arithmetic and copies ran while one was open for 1% of the time, Pallas kernels for 11%

profile of v2, /device:TPU:9, one launch (start us, length us, event | category | flops | bytes accessed | tf_op | source)
XLA Modules:
  0.0 154.3 jit_solution(3719784034551009252)
XLA Ops:
  0.6 4.0 %shard_map.85 = bf16[8,4,4,64,128]{4,3,2,1,0:T(8,128)(2,1)} custom-call(bf16[64,8192]{1,0:T(8,128)(2,1)} %refs_0_.3, bf16[64,8192]{1,0:T(8,128)(2,1)} %refs_1_.3, bf16[64,8192]{1,0:T(8,128)(2,1)} %refs_2_.3, bf16[64,8192]{1,0:T(8,128)(2,1)} %refs_3_.3), custom_call_target="tpu_custom_call" | custom-call | bytes 4194304 | tf_op jit(solution)/shard_map/pallas_call | solution.py:51
  4.6 6.4 %all-to-all-start = ((bf16[32,4,64,128]{3,2,1,0:T(8,128)(2,1)}), bf16[32,4,64,128]{3,2,1,0:T(8,128)(2,1)S(1)}, u32[]{:S(2)}, u32[]{:S(2)}) async-start(bf16[32,4,64,128]{3,2,1,0:T(8,128)(2,1)} %bitcast.9), calls=%async_computation | async-start | bytes 4194304 | tf_op jit(solution)/shard_map/all_to_all | solution.py:189
  11.0 4.0 %shard_map.84 = bf16[8,4,4,64,128]{4,3,2,1,0:T(8,128)(2,1)} custom-call(bf16[64,8192]{1,0:T(8,128)(2,1)} %refs_0_.3, bf16[64,8192]{1,0:T(8,128)(2,1)} %refs_1_.3, bf16[64,8192]{1,0:T(8,128)(2,1)} %refs_2_.3, bf16[64,8192]{1,0:T(8,128)(2,1)} %refs_3_.3), custom_call_target="tpu_custom_call" | custom-call | bytes 4194304 | tf_op jit(solution)/shard_map/pallas_call | solution.py:51
  15.0 1.8 %convert_reduce_fusion = s32[2048]{0:T(1024)S(1)} fusion(s32[2048]{0:T(1024)S(1)} %copy-done.2), kind=kLoop, calls=%fused_computation | loop fusion | flops 12580864 | bytes 16384 | tf_op jit(solution)/shard_map/reduce_sum | solution.py:180
  16.9 42.2 %all-to-all-done = bf16[32,4,64,128]{3,2,1,0:T(8,128)(2,1)S(1)} async-done(((bf16[32,4,64,128]{3,2,1,0:T(8,128)(2,1)}), bf16[32,4,64,128]{3,2,1,0:T(8,128)(2,1)S(1)}, u32[]{:S(2)}, u32[]{:S(2)}) %all-to-all-start) | async-done | bytes 2097184 | tf_op jit(solution)/shard_map/all_to_all | solution.py:189
  59.1 1.3 copy-done
  60.4 3.5 %all-to-all-start.1 = ((bf16[32,4,64,128]{3,2,1,0:T(8,128)(2,1)}), bf16[32,4,64,128]{3,2,1,0:T(8,128)(2,1)S(1)}, u32[]{:S(2)}, u32[]{:S(2)}) async-start(bf16[32,4,64,128]{3,2,1,0:T(8,128)(2,1)} %bitcast.8), calls=%async_computation.1 | async-start | bytes 4194304 | tf_op jit(solution)/shard_map/all_to_all | solution.py:189
  64.3 1.6 %copy-done.1 = bf16[32,4,64,128]{3,2,1,0:T(8,128)(2,1)S(1)} copy-done((bf16[32,4,64,128]{3,2,1,0:T(8,128)(2,1)S(1)}, bf16[32,4,64,128]{3,2,1,0:T(8,128)(2,1)}, u32[]{:S(2)}) %copy-start.1) | copy-done | bytes 2097176
  65.9 10.0 %shard_map.86 = (bf16[4,256,128]{2,1,0:T(8,128)(2,1)S(1)}, bf16[4,256,128]{2,1,0:T(8,128)(2,1)S(1)}, bf16[4,256,128]{2,1,0:T(8,128)(2,1)S(1)}, bf16[4,256,128]{2...) custom-call(s32[8]{0:T(128)S(1)} %subtract_add_fusion.count_ref, ...), custom_call_target="tpu_custom_call" | custom-call | flops 2415919104 | bytes 4194304 | tf_op jit(solution)/shard_map/pallas_call | solution.py:117
  75.9 2.1 %collective-permute-start.3 = (bf16[4,256,128]{2,1,0:T(8,128)(2,1)S(1)}, bf16[4,256,128]{2,1,0:T(8,128)(2,1)S(1)}, u32[]{:S(2)}, u32[]{:S(2)}) collective-permute-start(bf16[4,256,128]{2,1,0:T(8,128)(2,1)S(1)} %get-tuple-element.51), channel_id=1, source_target_pairs={{0,24},{4,28},{8,16},{12,20},{16,8},{20,12},{24,0},{28,4},{1,25},{... | collective-permute-start | bytes 786440 | tf_op jit(solution)/shard_map/ppermute | solution.py:168
  78.9 0.9 collective-permute-start
  80.1 1.2 collective-permute-start.6
  81.3 7.0 %collective-permute-done.3.refs_1_ = bf16[4,256,128]{2,1,0:T(8,128)(2,1)S(1)} collective-permute-done((bf16[4,256,128]{2,1,0:T(8,128)(2,1)S(1)}, bf16[4,256,128]{2,1,0:T(8,128)(2,1)S(1)}, u32[]{:S(2)}, u32[]{:S(2)}) %collective-permute-start.3) | collective-permute-done | bytes 262176 | tf_op jit(solution)/shard_map/ppermute | solution.py:168
  88.3 3.5 %collective-permute-start.1 = (bf16[4,256,128]{2,1,0:T(8,128)(2,1)S(1)}, bf16[4,256,128]{2,1,0:T(8,128)(2,1)S(1)}, u32[]{:S(2)}, u32[]{:S(2)}) collective-permute-start(bf16[4,256,128]{2,1,0:T(8,128)(2,1)S(1)} %get-tuple-element.48), channel_id=1, source_target_pairs={{0,20},{4,16},{8,28},{12,24},{16,4},{20,0},{24,12},{28,8},{1,21},{... | collective-permute-start | bytes 786440 | tf_op jit(solution)/shard_map/ppermute | solution.py:168
  91.8 10.7 %collective-permute-done.4.refs_2_ = bf16[4,256,128]{2,1,0:T(8,128)(2,1)S(1)} collective-permute-done((bf16[4,256,128]{2,1,0:T(8,128)(2,1)S(1)}, bf16[4,256,128]{2,1,0:T(8,128)(2,1)S(1)}, u32[]{:S(2)}, u32[]{:S(2)}) %collective-permute-start.4) | collective-permute-done | bytes 262176 | tf_op jit(solution)/shard_map/ppermute | solution.py:168
  102.5 12.3 %collective-permute-done.5.refs_3_ = bf16[4,256,128]{2,1,0:T(8,128)(2,1)S(1)} collective-permute-done((bf16[4,256,128]{2,1,0:T(8,128)(2,1)S(1)}, bf16[4,256,128]{2,1,0:T(8,128)(2,1)S(1)}, u32[]{:S(2)}, u32[]{:S(2)}) %collective-permute-start.5) | collective-permute-done | bytes 262176 | tf_op jit(solution)/shard_map/ppermute | solution.py:168
  114.8 1.2 shard_map.87
  116.0 1.0 shard_map.88
  117.0 10.0 %shard_map.89 = (bf16[4,256,128]{2,1,0:T(8,128)(2,1)S(1)}, bf16[4,256,128]{2,1,0:T(8,128)(2,1)S(1)}, bf16[4,256,128]{2,1,0:T(8,128)(2,1)S(1)}, bf16[4,256,128]{2...) custom-call(s32[8]{0:T(128)S(1)} %subtract_add_fusion.count_ref, ...), custom_call_target="tpu_custom_call" | custom-call | flops 2415919104 | bytes 4194304 | tf_op jit(solution)/shard_map/pallas_call | solution.py:117
  127.0 1.9 %collective-permute-start.10 = (bf16[4,256,128]{2,1,0:T(8,128)(2,1)S(1)}, bf16[4,256,128]{2,1,0:T(8,128)(2,1)S(1)}, u32[]{:S(2)}, u32[]{:S(2)}) collective-permute-start(bf16[4,256,128]{2,1,0:T(8,128)(2,1)S(1)} %get-tuple-element.68), channel_id=1, source_target_pairs={{0,24},{4,28},{8,16},{12,20},{16,8},{20,12},{24,0},{28,4},{1,25},{... | collective-permute-start | bytes 786440 | tf_op jit(solution)/shard_map/ppermute | solution.py:168
  128.9 1.5 collective-permute-start.11
  130.4 0.8 collective-permute-start.12
  131.2 1.3 collective-permute-start.13
  132.6 2.5 %collective-permute-done.10.refs_1_ = bf16[4,256,128]{2,1,0:T(8,128)(2,1)S(1)} collective-permute-done((bf16[4,256,128]{2,1,0:T(8,128)(2,1)S(1)}, bf16[4,256,128]{2,1,0:T(8,128)(2,1)S(1)}, u32[]{:S(2)}, u32[]{:S(2)}) %collective-permute-start.10) | collective-permute-done | bytes 262176 | tf_op jit(solution)/shard_map/ppermute | solution.py:168
  135.0 3.5 %collective-permute-start.8 = (bf16[4,256,128]{2,1,0:T(8,128)(2,1)S(1)}, bf16[4,256,128]{2,1,0:T(8,128)(2,1)S(1)}, u32[]{:S(2)}, u32[]{:S(2)}) collective-permute-start(bf16[4,256,128]{2,1,0:T(8,128)(2,1)S(1)} %get-tuple-element.65), channel_id=1, source_target_pairs={{0,20},{4,16},{8,28},{12,24},{16,4},{20,0},{24,12},{28,8},{1,21},{... | collective-permute-start | bytes 786440 | tf_op jit(solution)/shard_map/ppermute | solution.py:168
  138.5 4.4 %collective-permute-done.11.refs_2_ = bf16[4,256,128]{2,1,0:T(8,128)(2,1)S(1)} collective-permute-done((bf16[4,256,128]{2,1,0:T(8,128)(2,1)S(1)}, bf16[4,256,128]{2,1,0:T(8,128)(2,1)S(1)}, u32[]{:S(2)}, u32[]{:S(2)}) %collective-permute-start.11) | collective-permute-done | bytes 262176 | tf_op jit(solution)/shard_map/ppermute | solution.py:168
  142.9 2.1 %collective-permute-done.12.refs_3_ = bf16[4,256,128]{2,1,0:T(8,128)(2,1)S(1)} collective-permute-done((bf16[4,256,128]{2,1,0:T(8,128)(2,1)S(1)}, bf16[4,256,128]{2,1,0:T(8,128)(2,1)S(1)}, u32[]{:S(2)}, u32[]{:S(2)}) %collective-permute-start.12) | collective-permute-done | bytes 262176 | tf_op jit(solution)/shard_map/ppermute | solution.py:168
  145.1 2.4 %collective-permute-done.13.refs_4_ = bf16[4,256,128]{2,1,0:T(8,128)(2,1)S(1)} collective-permute-done((bf16[4,256,128]{2,1,0:T(8,128)(2,1)S(1)}, bf16[4,256,128]{2,1,0:T(8,128)(2,1)S(1)}, u32[]{:S(2)}, u32[]{:S(2)}) %collective-permute-start.13) | collective-permute-done | bytes 262176 | tf_op jit(solution)/shard_map/ppermute | solution.py:168
  147.5 1.2 shard_map.90
  148.7 3.6 %collective-permute-done.7.refs_0_ = bf16[4,256,128]{2,1,0:T(8,128)(2,1)S(1)} collective-permute-done((bf16[4,256,128]{2,1,0:T(8,128)(2,1)S(1)}, bf16[4,256,128]{2,1,0:T(8,128)(2,1)S(1)}, u32[]{:S(2)}, u32[]{:S(2)}) %collective-permute-start.7) | collective-permute-done | bytes 262176 | tf_op jit(solution)/shard_map/ppermute | solution.py:168
  152.3 0.8 collective-permute-done.8.refs_1_
  153.1 1.0 shard_map.91
  (19 shorter events, 1.6 us)
Async XLA Ops:
  4.6 54.5 %all-to-all-start = ((bf16[32,4,64,128]{3,2,1,0:T(8,128)(2,1)}), bf16[32,4,64,128]{3,2,1,0:T(8,128)(2,1)S(1)}, u32[]{:S(2)}, u32[]{:S(2)}) async-start(bf16[32,4,64,128]{3,2,1,0:T(8,128)(2,1)} %bitcast.9), calls=%async_computation | async-start | bytes 4194304 | tf_op jit(solution)/shard_map/all_to_all | solution.py:189
  10.9 4.0 %copy-start.2 = (s32[2048]{0:T(1024)S(1)}, s32[2048]{0:T(1024)}, u32[]{:S(2)}) copy-start(s32[2048]{0:T(1024)} %param.5) | copy-start | bytes 24580
  59.1 1.3 copy-start
  60.4 56.6 %all-to-all-start.1 = ((bf16[32,4,64,128]{3,2,1,0:T(8,128)(2,1)}), bf16[32,4,64,128]{3,2,1,0:T(8,128)(2,1)S(1)}, u32[]{:S(2)}, u32[]{:S(2)}) async-start(bf16[32,4,64,128]{3,2,1,0:T(8,128)(2,1)} %bitcast.8), calls=%async_computation.1 | async-start | bytes 4194304 | tf_op jit(solution)/shard_map/all_to_all | solution.py:189
  64.3 1.6 %copy-start.1 = (bf16[32,4,64,128]{3,2,1,0:T(8,128)(2,1)S(1)}, bf16[32,4,64,128]{3,2,1,0:T(8,128)(2,1)}, u32[]{:S(2)}) copy-start(bf16[32,4,64,128]{3,2,1,0:T(8,128)(2,1)} %copy-done) | copy-start | bytes 6291460
  75.9 12.3 %collective-permute-start.3 = (bf16[4,256,128]{2,1,0:T(8,128)(2,1)S(1)}, bf16[4,256,128]{2,1,0:T(8,128)(2,1)S(1)}, u32[]{:S(2)}, u32[]{:S(2)}) collective-permute-start(bf16[4,256,128]{2,1,0:T(8,128)(2,1)S(1)} %get-tuple-element.51), channel_id=1, source_target_pairs={{0,24},{4,28},{8,16},{12,20},{16,8},{20,12},{24,0},{28,4},{1,25},{... | collective-permute-start | bytes 786440 | tf_op jit(solution)/shard_map/ppermute | solution.py:168
  78.1 24.4 %collective-permute-start.4 = (bf16[4,256,128]{2,1,0:T(8,128)(2,1)S(1)}, bf16[4,256,128]{2,1,0:T(8,128)(2,1)S(1)}, u32[]{:S(2)}, u32[]{:S(2)}) collective-permute-start(bf16[4,256,128]{2,1,0:T(8,128)(2,1)S(1)} %get-tuple-element.52), channel_id=1, source_target_pairs={{0,28},{4,24},{8,20},{12,16},{16,12},{20,8},{24,4},{28,0},{1,29},{... | collective-permute-start | bytes 786440 | tf_op jit(solution)/shard_map/ppermute | solution.py:168
  78.9 37.1 %collective-permute-start = (bf16[4,256,128]{2,1,0:T(8,128)(2,1)S(1)}, bf16[4,256,128]{2,1,0:T(8,128)(2,1)S(1)}, u32[]{:S(2)}, u32[]{:S(2)}) collective-permute-start(bf16[4,256,128]{2,1,0:T(8,128)(2,1)S(1)} %get-tuple-element.47), channel_id=1, source_target_pairs={{0,12},{4,8},{8,4},{12,0},{16,28},{20,24},{24,20},{28,16},{1,13},{... | collective-permute-start | bytes 786440 | tf_op jit(solution)/shard_map/ppermute | solution.py:168
  79.8 35.0 %collective-permute-start.5 = (bf16[4,256,128]{2,1,0:T(8,128)(2,1)S(1)}, bf16[4,256,128]{2,1,0:T(8,128)(2,1)S(1)}, u32[]{:S(2)}, u32[]{:S(2)}) collective-permute-start(bf16[4,256,128]{2,1,0:T(8,128)(2,1)S(1)} %get-tuple-element.53), channel_id=1, source_target_pairs={{0,8},{4,12},{8,0},{12,4},{16,24},{20,28},{24,16},{28,20},{1,9},{5... | collective-permute-start | bytes 786440 | tf_op jit(solution)/shard_map/ppermute | solution.py:168
  80.1 34.7 %collective-permute-start.6 = (bf16[4,256,128]{2,1,0:T(8,128)(2,1)S(1)}, bf16[4,256,128]{2,1,0:T(8,128)(2,1)S(1)}, u32[]{:S(2)}, u32[]{:S(2)}) collective-permute-start(bf16[4,256,128]{2,1,0:T(8,128)(2,1)S(1)} %get-tuple-element.54), channel_id=1, source_target_pairs={{0,16},{4,20},{8,24},{12,28},{16,0},{20,4},{24,8},{28,12},{1,17},{... | collective-permute-start | bytes 786440 | tf_op jit(solution)/shard_map/ppermute | solution.py:168
  88.3 27.7 %collective-permute-start.1 = (bf16[4,256,128]{2,1,0:T(8,128)(2,1)S(1)}, bf16[4,256,128]{2,1,0:T(8,128)(2,1)S(1)}, u32[]{:S(2)}, u32[]{:S(2)}) collective-permute-start(bf16[4,256,128]{2,1,0:T(8,128)(2,1)S(1)} %get-tuple-element.48), channel_id=1, source_target_pairs={{0,20},{4,16},{8,28},{12,24},{16,4},{20,0},{24,12},{28,8},{1,21},{... | collective-permute-start | bytes 786440 | tf_op jit(solution)/shard_map/ppermute | solution.py:168
  102.5 13.6 %collective-permute-start.2 = (bf16[4,256,128]{2,1,0:T(8,128)(2,1)S(1)}, bf16[4,256,128]{2,1,0:T(8,128)(2,1)S(1)}, u32[]{:S(2)}, u32[]{:S(2)}) collective-permute-start(bf16[4,256,128]{2,1,0:T(8,128)(2,1)S(1)} %get-tuple-element.49), channel_id=1, source_target_pairs={{0,4},{4,0},{8,12},{12,8},{16,20},{20,16},{24,28},{28,24},{1,5},{5... | collective-permute-start | bytes 786440 | tf_op jit(solution)/shard_map/ppermute | solution.py:168
  127.0 8.0 %collective-permute-start.10 = (bf16[4,256,128]{2,1,0:T(8,128)(2,1)S(1)}, bf16[4,256,128]{2,1,0:T(8,128)(2,1)S(1)}, u32[]{:S(2)}, u32[]{:S(2)}) collective-permute-start(bf16[4,256,128]{2,1,0:T(8,128)(2,1)S(1)} %get-tuple-element.68), channel_id=1, source_target_pairs={{0,24},{4,28},{8,16},{12,20},{16,8},{20,12},{24,0},{28,4},{1,25},{... | collective-permute-start | bytes 786440 | tf_op jit(solution)/shard_map/ppermute | solution.py:168
  128.9 14.1 %collective-permute-start.11 = (bf16[4,256,128]{2,1,0:T(8,128)(2,1)S(1)}, bf16[4,256,128]{2,1,0:T(8,128)(2,1)S(1)}, u32[]{:S(2)}, u32[]{:S(2)}) collective-permute-start(bf16[4,256,128]{2,1,0:T(8,128)(2,1)S(1)} %get-tuple-element.69), channel_id=1, source_target_pairs={{0,28},{4,24},{8,20},{12,16},{16,12},{20,8},{24,4},{28,0},{1,29},{... | collective-permute-start | bytes 786440 | tf_op jit(solution)/shard_map/ppermute | solution.py:168
  130.4 14.7 %collective-permute-start.12 = (bf16[4,256,128]{2,1,0:T(8,128)(2,1)S(1)}, bf16[4,256,128]{2,1,0:T(8,128)(2,1)S(1)}, u32[]{:S(2)}, u32[]{:S(2)}) collective-permute-start(bf16[4,256,128]{2,1,0:T(8,128)(2,1)S(1)} %get-tuple-element.70), channel_id=1, source_target_pairs={{0,8},{4,12},{8,0},{12,4},{16,24},{20,28},{24,16},{28,20},{1,9},{5... | collective-permute-start | bytes 786440 | tf_op jit(solution)/shard_map/ppermute | solution.py:168
  131.2 16.3 %collective-permute-start.13 = (bf16[4,256,128]{2,1,0:T(8,128)(2,1)S(1)}, bf16[4,256,128]{2,1,0:T(8,128)(2,1)S(1)}, u32[]{:S(2)}, u32[]{:S(2)}) collective-permute-start(bf16[4,256,128]{2,1,0:T(8,128)(2,1)S(1)} %get-tuple-element.71), channel_id=1, source_target_pairs={{0,16},{4,20},{8,24},{12,28},{16,0},{20,4},{24,8},{28,12},{1,17},{... | collective-permute-start | bytes 786440 | tf_op jit(solution)/shard_map/ppermute | solution.py:168
  132.6 19.7 %collective-permute-start.7 = (bf16[4,256,128]{2,1,0:T(8,128)(2,1)S(1)}, bf16[4,256,128]{2,1,0:T(8,128)(2,1)S(1)}, u32[]{:S(2)}, u32[]{:S(2)}) collective-permute-start(bf16[4,256,128]{2,1,0:T(8,128)(2,1)S(1)} %get-tuple-element.64), channel_id=1, source_target_pairs={{0,12},{4,8},{8,4},{12,0},{16,28},{20,24},{24,20},{28,16},{1,13},{... | collective-permute-start | bytes 786440 | tf_op jit(solution)/shard_map/ppermute | solution.py:168
  135.0 18.1 %collective-permute-start.8 = (bf16[4,256,128]{2,1,0:T(8,128)(2,1)S(1)}, bf16[4,256,128]{2,1,0:T(8,128)(2,1)S(1)}, u32[]{:S(2)}, u32[]{:S(2)}) collective-permute-start(bf16[4,256,128]{2,1,0:T(8,128)(2,1)S(1)} %get-tuple-element.65), channel_id=1, source_target_pairs={{0,20},{4,16},{8,28},{12,24},{16,4},{20,0},{24,12},{28,8},{1,21},{... | collective-permute-start | bytes 786440 | tf_op jit(solution)/shard_map/ppermute | solution.py:168
  142.9 10.2 %collective-permute-start.9 = (bf16[4,256,128]{2,1,0:T(8,128)(2,1)S(1)}, bf16[4,256,128]{2,1,0:T(8,128)(2,1)S(1)}, u32[]{:S(2)}, u32[]{:S(2)}) collective-permute-start(bf16[4,256,128]{2,1,0:T(8,128)(2,1)S(1)} %get-tuple-element.66), channel_id=1, source_target_pairs={{0,4},{4,0},{8,12},{12,8},{16,20},{20,16},{24,28},{28,24},{1,5},{5... | collective-permute-start | bytes 786440 | tf_op jit(solution)/shard_map/ppermute | solution.py:168

commit v3 on v2

--- a/solution.py
+++ b/solution.py
@@ -54,6 +54,7 @@
         out_shape=low_array(owners, chans, 4, rows, HEAD_DIM),
         in_specs=[pl.BlockSpec((rows, owners * HEAD_DIM), lambda c: (0, c * turns + turn))] * 4,
         out_specs=pl.BlockSpec((owners, 1, 4, rows, HEAD_DIM), lambda c: (0, c, 0, 0, 0)),
+        compiler_params=pltpu.CompilerParams(vmem_limit_bytes=8 << 20),
         cost_estimate=moved(16 * rows * width // turns),
     )(*inputs)
 

time: 155 us -> 157 us (1.013)
  Pallas kernels: 32.3 us -> 28.4 us
  local copies, waits for them, and re-layouts: 3.34 us -> 6.58 us
    pallas_call x2, Pallas kernels: 7.96 us -> 4.27 us  [pack(): pl.pallas_call(functools.partial(pack_kernel, owners), grid=(chans,), out...]
    unnamed x6 -> x18, local copies, waits for them, and re-layouts: 2.89 us -> 6.13 us
  transfers between devices with their start and end apart: 16 -> 16, of which waited for: 10 -> 9; matrix products, arithmetic and copies ran while one was open for 1% -> 1% of each run, Pallas kernels for 11% -> 10%
where the time goes in v3:
time: 157 us; the launch traced here: 155 us
  waiting for transfers between devices  88.6 us (56%)
  starting transfers between devices  28.5 us (18%)
  Pallas kernels  28.4 us (18%)
  local copies, waits for them, and re-layouts  6.58 us (4%)
  other arithmetic  1.81 us (1%)
    ppermute x14, waiting for transfers between devices, exchange(): lax.ppermute(value, 'seq', [(s, s ^ d) for s in range(lax.axis_size('seq'...  45.7 us
    all_to_all x2, waiting for transfers between devices, gather(): lax.all_to_all(parts, ('seq', 'chan'), split_axis=0, concat_axis=0, tiled...  42.9 us
    pallas_call x2, Pallas kernels, attention(): pl.pallas_call(functools.partial(attention_kernel, spans), out_shape=[low...  19.8 us
    ppermute x14, starting transfers between devices, exchange(): lax.ppermute(value, 'seq', [(s, s ^ d) for s in range(lax.axis_size('seq'...  18.6 us
    all_to_all x2, starting transfers between devices, gather(): lax.all_to_all(parts, ('seq', 'chan'), split_axis=0, concat_axis=0, tiled...  9.92 us
    unnamed x18, local copies, waits for them, and re-layouts  6.13 us
    pallas_call x4, Pallas kernels, unpack(): pl.pallas_call(functools.partial(unpack_kernel, peers, base), out_shape=[...  4.36 us
    pallas_call x2, Pallas kernels, pack(): pl.pallas_call(functools.partial(pack_kernel, owners), grid=(chans,), out...  4.27 us
  transfers between devices with their start and end apart: 16, of which 9 were waited for; matrix products, arithmetic and copies ran while one was open for 1% of the time, Pallas kernels for 10%

profile of v3, /device:TPU:9, one launch (start us, length us, event | category | flops | bytes accessed | tf_op | source)
XLA Modules:
  0.0 154.9 jit_solution(5759699065450885603)
XLA Ops:
  0.6 1.2 copy-done
  1.9 1.2 copy-done.2
  3.1 1.2 copy-done.4
  4.3 1.2 copy-done.6
  5.5 2.1 %shard_map.85 = bf16[8,4,4,64,128]{4,3,2,1,0:T(8,128)(2,1)} custom-call(bf16[64,8192]{1,0:T(8,128)(2,1)S(1)} %copy-done, bf16[64,8192]{1,0:T(8,128)(2,1)S(1)} %copy-done.2, bf16[64,8192]{1,0:T(8,128)(2,1)S(1)} %copy-done.4, bf16[64,8192]{1,0:T(8,128)(2,1)S(1)} %copy-done.6), custom_call_target="tpu_custom_call" | custom-call | bytes 4194304 | tf_op jit(solution)/shard_map/pallas_call | solution.py:51
  7.7 6.4 %all-to-all-start = ((bf16[32,4,64,128]{3,2,1,0:T(8,128)(2,1)}), bf16[32,4,64,128]{3,2,1,0:T(8,128)(2,1)}, u32[]{:S(2)}, u32[]{:S(2)}) async-start(bf16[32,4,64,128]{3,2,1,0:T(8,128)(2,1)} %bitcast.2), calls=%async_computation | async-start | bytes 4194304 | tf_op jit(solution)/shard_map/all_to_all | solution.py:190
  14.2 1.2 copy-done.7
  15.4 2.1 %shard_map.84 = bf16[8,4,4,64,128]{4,3,2,1,0:T(8,128)(2,1)} custom-call(bf16[64,8192]{1,0:T(8,128)(2,1)S(1)} %copy-done.1, bf16[64,8192]{1,0:T(8,128)(2,1)S(1)} %copy-done.3, bf16[64,8192]{1,0:T(8,128)(2,1)S(1)} %copy-done.5, bf16[64,8192]{1,0:T(8,128)(2,1)S(1)} %copy-done.7), custom_call_target="tpu_custom_call" | custom-call | bytes 4194304 | tf_op jit(solution)/shard_map/pallas_call | solution.py:51
  17.5 1.8 %convert_reduce_fusion = s32[2048]{0:T(1024)S(1)} fusion(s32[2048]{0:T(1024)S(1)} %copy-done.8), kind=kLoop, calls=%fused_computation | loop fusion | flops 12580864 | bytes 16384 | tf_op jit(solution)/shard_map/reduce_sum | solution.py:181
  19.4 42.9 %all-to-all-done = bf16[32,4,64,128]{3,2,1,0:T(8,128)(2,1)} async-done(((bf16[32,4,64,128]{3,2,1,0:T(8,128)(2,1)}), bf16[32,4,64,128]{3,2,1,0:T(8,128)(2,1)}, u32[]{:S(2)}, u32[]{:S(2)}) %all-to-all-start) | async-done | bytes 2097184 | tf_op jit(solution)/shard_map/all_to_all | solution.py:190
  62.3 3.5 %all-to-all-start.1 = ((bf16[32,4,64,128]{3,2,1,0:T(8,128)(2,1)}), bf16[32,4,64,128]{3,2,1,0:T(8,128)(2,1)S(1)}, u32[]{:S(2)}, u32[]{:S(2)}) async-start(bf16[32,4,64,128]{3,2,1,0:T(8,128)(2,1)} %bitcast.4), calls=%async_computation.1 | async-start | bytes 4194304 | tf_op jit(solution)/shard_map/all_to_all | solution.py:190
  66.2 10.4 %shard_map.86 = (bf16[4,256,128]{2,1,0:T(8,128)(2,1)S(1)}, bf16[4,256,128]{2,1,0:T(8,128)(2,1)S(1)}, bf16[4,256,128]{2,1,0:T(8,128)(2,1)S(1)}, bf16[4,256,128]{2...) custom-call(s32[8]{0:T(128)S(1)} %subtract_add_fusion.count_ref, ...), custom_call_target="tpu_custom_call" | custom-call | flops 2415919104 | bytes 4194304 | tf_op jit(solution)/shard_map/pallas_call | solution.py:118
  76.6 2.2 %collective-permute-start.3 = (bf16[4,256,128]{2,1,0:T(8,128)(2,1)S(1)}, bf16[4,256,128]{2,1,0:T(8,128)(2,1)S(1)}, u32[]{:S(2)}, u32[]{:S(2)}) collective-permute-start(bf16[4,256,128]{2,1,0:T(8,128)(2,1)S(1)} %get-tuple-element.51), channel_id=1, source_target_pairs={{0,24},{4,28},{8,16},{12,20},{16,8},{20,12},{24,0},{28,4},{1,25},{... | collective-permute-start | bytes 786440 | tf_op jit(solution)/shard_map/ppermute | solution.py:169
  80.8 1.2 collective-permute-start.6
  82.0 8.9 %collective-permute-done.3.refs_1_ = bf16[4,256,128]{2,1,0:T(8,128)(2,1)S(1)} collective-permute-done((bf16[4,256,128]{2,1,0:T(8,128)(2,1)S(1)}, bf16[4,256,128]{2,1,0:T(8,128)(2,1)S(1)}, u32[]{:S(2)}, u32[]{:S(2)}) %collective-permute-start.3) | collective-permute-done | bytes 262176 | tf_op jit(solution)/shard_map/ppermute | solution.py:169
  90.9 1.7 %collective-permute-start.1 = (bf16[4,256,128]{2,1,0:T(8,128)(2,1)S(1)}, bf16[4,256,128]{2,1,0:T(8,128)(2,1)S(1)}, u32[]{:S(2)}, u32[]{:S(2)}) collective-permute-start(bf16[4,256,128]{2,1,0:T(8,128)(2,1)S(1)} %get-tuple-element.48), channel_id=1, source_target_pairs={{0,20},{4,16},{8,28},{12,24},{16,4},{20,0},{24,12},{28,8},{1,21},{... | collective-permute-start | bytes 786440 | tf_op jit(solution)/shard_map/ppermute | solution.py:169
  92.6 11.1 %collective-permute-done.4.refs_2_ = bf16[4,256,128]{2,1,0:T(8,128)(2,1)S(1)} collective-permute-done((bf16[4,256,128]{2,1,0:T(8,128)(2,1)S(1)}, bf16[4,256,128]{2,1,0:T(8,128)(2,1)S(1)}, u32[]{:S(2)}, u32[]{:S(2)}) %collective-permute-start.4) | collective-permute-done | bytes 262176 | tf_op jit(solution)/shard_map/ppermute | solution.py:169
  104.0 11.6 %collective-permute-done.5.refs_3_ = bf16[4,256,128]{2,1,0:T(8,128)(2,1)S(1)} collective-permute-done((bf16[4,256,128]{2,1,0:T(8,128)(2,1)S(1)}, bf16[4,256,128]{2,1,0:T(8,128)(2,1)S(1)}, u32[]{:S(2)}, u32[]{:S(2)}) %collective-permute-start.5) | collective-permute-done | bytes 262176 | tf_op jit(solution)/shard_map/ppermute | solution.py:169
  115.7 1.2 shard_map.87
  116.9 1.0 shard_map.88
  117.9 9.4 %shard_map.89 = (bf16[4,256,128]{2,1,0:T(8,128)(2,1)S(1)}, bf16[4,256,128]{2,1,0:T(8,128)(2,1)S(1)}, bf16[4,256,128]{2,1,0:T(8,128)(2,1)S(1)}, bf16[4,256,128]{2...) custom-call(s32[8]{0:T(128)S(1)} %subtract_add_fusion.count_ref, ...), custom_call_target="tpu_custom_call" | custom-call | flops 2415919104 | bytes 4194304 | tf_op jit(solution)/shard_map/pallas_call | solution.py:118
  127.3 1.6 %collective-permute-start.10 = (bf16[4,256,128]{2,1,0:T(8,128)(2,1)S(1)}, bf16[4,256,128]{2,1,0:T(8,128)(2,1)S(1)}, u32[]{:S(2)}, u32[]{:S(2)}) collective-permute-start(bf16[4,256,128]{2,1,0:T(8,128)(2,1)S(1)} %get-tuple-element.68), channel_id=1, source_target_pairs={{0,24},{4,28},{8,16},{12,20},{16,8},{20,12},{24,0},{28,4},{1,25},{... | collective-permute-start | bytes 786440 | tf_op jit(solution)/shard_map/ppermute | solution.py:169
  128.8 2.1 %collective-permute-start.11 = (bf16[4,256,128]{2,1,0:T(8,128)(2,1)S(1)}, bf16[4,256,128]{2,1,0:T(8,128)(2,1)S(1)}, u32[]{:S(2)}, u32[]{:S(2)}) collective-permute-start(bf16[4,256,128]{2,1,0:T(8,128)(2,1)S(1)} %get-tuple-element.69), channel_id=1, source_target_pairs={{0,28},{4,24},{8,20},{12,16},{16,12},{20,8},{24,4},{28,0},{1,29},{... | collective-permute-start | bytes 786440 | tf_op jit(solution)/shard_map/ppermute | solution.py:169
  130.9 1.6 %collective-permute-start.12 = (bf16[4,256,128]{2,1,0:T(8,128)(2,1)S(1)}, bf16[4,256,128]{2,1,0:T(8,128)(2,1)S(1)}, u32[]{:S(2)}, u32[]{:S(2)}) collective-permute-start(bf16[4,256,128]{2,1,0:T(8,128)(2,1)S(1)} %get-tuple-element.70), channel_id=1, source_target_pairs={{0,8},{4,12},{8,0},{12,4},{16,24},{20,28},{24,16},{28,20},{1,9},{5... | collective-permute-start | bytes 786440 | tf_op jit(solution)/shard_map/ppermute | solution.py:169
  132.9 0.9 collective-permute-start.7
  133.8 1.2 collective-permute-done.10.refs_1_
  135.0 4.6 %collective-permute-start.8 = (bf16[4,256,128]{2,1,0:T(8,128)(2,1)S(1)}, bf16[4,256,128]{2,1,0:T(8,128)(2,1)S(1)}, u32[]{:S(2)}, u32[]{:S(2)}) collective-permute-start(bf16[4,256,128]{2,1,0:T(8,128)(2,1)S(1)} %get-tuple-element.65), channel_id=1, source_target_pairs={{0,20},{4,16},{8,28},{12,24},{16,4},{20,0},{24,12},{28,8},{1,21},{... | collective-permute-start | bytes 786440 | tf_op jit(solution)/shard_map/ppermute | solution.py:169
  139.6 3.9 %collective-permute-done.11.refs_2_ = bf16[4,256,128]{2,1,0:T(8,128)(2,1)S(1)} collective-permute-done((bf16[4,256,128]{2,1,0:T(8,128)(2,1)S(1)}, bf16[4,256,128]{2,1,0:T(8,128)(2,1)S(1)}, u32[]{:S(2)}, u32[]{:S(2)}) %collective-permute-start.11) | collective-permute-done | bytes 262176 | tf_op jit(solution)/shard_map/ppermute | solution.py:169
  143.5 4.0 %collective-permute-done.12.refs_3_ = bf16[4,256,128]{2,1,0:T(8,128)(2,1)S(1)} collective-permute-done((bf16[4,256,128]{2,1,0:T(8,128)(2,1)S(1)}, bf16[4,256,128]{2,1,0:T(8,128)(2,1)S(1)}, u32[]{:S(2)}, u32[]{:S(2)}) %collective-permute-start.12) | collective-permute-done | bytes 262176 | tf_op jit(solution)/shard_map/ppermute | solution.py:169
  147.8 1.2 shard_map.90
  149.0 4.8 %collective-permute-done.7.refs_0_ = bf16[4,256,128]{2,1,0:T(8,128)(2,1)S(1)} collective-permute-done((bf16[4,256,128]{2,1,0:T(8,128)(2,1)S(1)}, bf16[4,256,128]{2,1,0:T(8,128)(2,1)S(1)}, u32[]{:S(2)}, u32[]{:S(2)}) %collective-permute-start.7) | collective-permute-done | bytes 262176 | tf_op jit(solution)/shard_map/ppermute | solution.py:169
  153.8 1.0 shard_map.91
  (31 shorter events, 3.4 us)
Async XLA Ops:
  0.6 1.2 copy-start
  1.9 1.2 copy-start.2
  3.1 1.2 copy-start.4
  4.3 1.2 copy-start.6
  7.7 6.4 %copy-start.1 = (bf16[64,8192]{1,0:T(8,128)(2,1)S(1)}, bf16[64,8192]{1,0:T(8,128)(2,1)}, u32[]{:S(2)}) copy-start(bf16[64,8192]{1,0:T(8,128)(2,1)} %refs_0_.3) | copy-start | bytes 3145732
  7.7 6.4 %copy-start.3 = (bf16[64,8192]{1,0:T(8,128)(2,1)S(1)}, bf16[64,8192]{1,0:T(8,128)(2,1)}, u32[]{:S(2)}) copy-start(bf16[64,8192]{1,0:T(8,128)(2,1)} %refs_1_.3) | copy-start | bytes 3145732
  7.7 6.4 %copy-start.5 = (bf16[64,8192]{1,0:T(8,128)(2,1)S(1)}, bf16[64,8192]{1,0:T(8,128)(2,1)}, u32[]{:S(2)}) copy-start(bf16[64,8192]{1,0:T(8,128)(2,1)} %refs_2_.3) | copy-start | bytes 3145732
  7.7 54.6 %all-to-all-start = ((bf16[32,4,64,128]{3,2,1,0:T(8,128)(2,1)}), bf16[32,4,64,128]{3,2,1,0:T(8,128)(2,1)}, u32[]{:S(2)}, u32[]{:S(2)}) async-start(bf16[32,4,64,128]{3,2,1,0:T(8,128)(2,1)} %bitcast.2), calls=%async_computation | async-start | bytes 4194304 | tf_op jit(solution)/shard_map/all_to_all | solution.py:190
  14.1 1.2 copy-start.7
  15.4 2.1 %copy-start.8 = (s32[2048]{0:T(1024)S(1)}, s32[2048]{0:T(1024)}, u32[]{:S(2)}) copy-start(s32[2048]{0:T(1024)} %param.5) | copy-start | bytes 24580
  62.3 55.6 %all-to-all-start.1 = ((bf16[32,4,64,128]{3,2,1,0:T(8,128)(2,1)}), bf16[32,4,64,128]{3,2,1,0:T(8,128)(2,1)S(1)}, u32[]{:S(2)}, u32[]{:S(2)}) async-start(bf16[32,4,64,128]{3,2,1,0:T(8,128)(2,1)} %bitcast.4), calls=%async_computation.1 | async-start | bytes 4194304 | tf_op jit(solution)/shard_map/all_to_all | solution.py:190
  76.6 14.2 %collective-permute-start.3 = (bf16[4,256,128]{2,1,0:T(8,128)(2,1)S(1)}, bf16[4,256,128]{2,1,0:T(8,128)(2,1)S(1)}, u32[]{:S(2)}, u32[]{:S(2)}) collective-permute-start(bf16[4,256,128]{2,1,0:T(8,128)(2,1)S(1)} %get-tuple-element.51), channel_id=1, source_target_pairs={{0,24},{4,28},{8,16},{12,20},{16,8},{20,12},{24,0},{28,4},{1,25},{... | collective-permute-start | bytes 786440 | tf_op jit(solution)/shard_map/ppermute | solution.py:169
  78.8 24.9 %collective-permute-start.4 = (bf16[4,256,128]{2,1,0:T(8,128)(2,1)S(1)}, bf16[4,256,128]{2,1,0:T(8,128)(2,1)S(1)}, u32[]{:S(2)}, u32[]{:S(2)}) collective-permute-start(bf16[4,256,128]{2,1,0:T(8,128)(2,1)S(1)} %get-tuple-element.52), channel_id=1, source_target_pairs={{0,28},{4,24},{8,20},{12,16},{16,12},{20,8},{24,4},{28,0},{1,29},{... | collective-permute-start | bytes 786440 | tf_op jit(solution)/shard_map/ppermute | solution.py:169
  79.6 37.3 %collective-permute-start = (bf16[4,256,128]{2,1,0:T(8,128)(2,1)S(1)}, bf16[4,256,128]{2,1,0:T(8,128)(2,1)S(1)}, u32[]{:S(2)}, u32[]{:S(2)}) collective-permute-start(bf16[4,256,128]{2,1,0:T(8,128)(2,1)S(1)} %get-tuple-element.47), channel_id=1, source_target_pairs={{0,12},{4,8},{8,4},{12,0},{16,28},{20,24},{24,20},{28,16},{1,13},{... | collective-permute-start | bytes 786440 | tf_op jit(solution)/shard_map/ppermute | solution.py:169
  80.5 35.1 %collective-permute-start.5 = (bf16[4,256,128]{2,1,0:T(8,128)(2,1)S(1)}, bf16[4,256,128]{2,1,0:T(8,128)(2,1)S(1)}, u32[]{:S(2)}, u32[]{:S(2)}) collective-permute-start(bf16[4,256,128]{2,1,0:T(8,128)(2,1)S(1)} %get-tuple-element.53), channel_id=1, source_target_pairs={{0,8},{4,12},{8,0},{12,4},{16,24},{20,28},{24,16},{28,20},{1,9},{5... | collective-permute-start | bytes 786440 | tf_op jit(solution)/shard_map/ppermute | solution.py:169
  80.8 34.8 %collective-permute-start.6 = (bf16[4,256,128]{2,1,0:T(8,128)(2,1)S(1)}, bf16[4,256,128]{2,1,0:T(8,128)(2,1)S(1)}, u32[]{:S(2)}, u32[]{:S(2)}) collective-permute-start(bf16[4,256,128]{2,1,0:T(8,128)(2,1)S(1)} %get-tuple-element.54), channel_id=1, source_target_pairs={{0,16},{4,20},{8,24},{12,28},{16,0},{20,4},{24,8},{28,12},{1,17},{... | collective-permute-start | bytes 786440 | tf_op jit(solution)/shard_map/ppermute | solution.py:169
  90.9 26.0 %collective-permute-start.1 = (bf16[4,256,128]{2,1,0:T(8,128)(2,1)S(1)}, bf16[4,256,128]{2,1,0:T(8,128)(2,1)S(1)}, u32[]{:S(2)}, u32[]{:S(2)}) collective-permute-start(bf16[4,256,128]{2,1,0:T(8,128)(2,1)S(1)} %get-tuple-element.48), channel_id=1, source_target_pairs={{0,20},{4,16},{8,28},{12,24},{16,4},{20,0},{24,12},{28,8},{1,21},{... | collective-permute-start | bytes 786440 | tf_op jit(solution)/shard_map/ppermute | solution.py:169
  103.7 13.2 %collective-permute-start.2 = (bf16[4,256,128]{2,1,0:T(8,128)(2,1)S(1)}, bf16[4,256,128]{2,1,0:T(8,128)(2,1)S(1)}, u32[]{:S(2)}, u32[]{:S(2)}) collective-permute-start(bf16[4,256,128]{2,1,0:T(8,128)(2,1)S(1)} %get-tuple-element.49), channel_id=1, source_target_pairs={{0,4},{4,0},{8,12},{12,8},{16,20},{20,16},{24,28},{28,24},{1,5},{5... | collective-permute-start | bytes 786440 | tf_op jit(solution)/shard_map/ppermute | solution.py:169
  127.3 7.7 %collective-permute-start.10 = (bf16[4,256,128]{2,1,0:T(8,128)(2,1)S(1)}, bf16[4,256,128]{2,1,0:T(8,128)(2,1)S(1)}, u32[]{:S(2)}, u32[]{:S(2)}) collective-permute-start(bf16[4,256,128]{2,1,0:T(8,128)(2,1)S(1)} %get-tuple-element.68), channel_id=1, source_target_pairs={{0,24},{4,28},{8,16},{12,20},{16,8},{20,12},{24,0},{28,4},{1,25},{... | collective-permute-start | bytes 786440 | tf_op jit(solution)/shard_map/ppermute | solution.py:169
  128.8 14.7 %collective-permute-start.11 = (bf16[4,256,128]{2,1,0:T(8,128)(2,1)S(1)}, bf16[4,256,128]{2,1,0:T(8,128)(2,1)S(1)}, u32[]{:S(2)}, u32[]{:S(2)}) collective-permute-start(bf16[4,256,128]{2,1,0:T(8,128)(2,1)S(1)} %get-tuple-element.69), channel_id=1, source_target_pairs={{0,28},{4,24},{8,20},{12,16},{16,12},{20,8},{24,4},{28,0},{1,29},{... | collective-permute-start | bytes 786440 | tf_op jit(solution)/shard_map/ppermute | solution.py:169
  130.9 16.6 %collective-permute-start.12 = (bf16[4,256,128]{2,1,0:T(8,128)(2,1)S(1)}, bf16[4,256,128]{2,1,0:T(8,128)(2,1)S(1)}, u32[]{:S(2)}, u32[]{:S(2)}) collective-permute-start(bf16[4,256,128]{2,1,0:T(8,128)(2,1)S(1)} %get-tuple-element.70), channel_id=1, source_target_pairs={{0,8},{4,12},{8,0},{12,4},{16,24},{20,28},{24,16},{28,20},{1,9},{5... | collective-permute-start | bytes 786440 | tf_op jit(solution)/shard_map/ppermute | solution.py:169
  132.6 15.2 %collective-permute-start.13 = (bf16[4,256,128]{2,1,0:T(8,128)(2,1)S(1)}, bf16[4,256,128]{2,1,0:T(8,128)(2,1)S(1)}, u32[]{:S(2)}, u32[]{:S(2)}) collective-permute-start(bf16[4,256,128]{2,1,0:T(8,128)(2,1)S(1)} %get-tuple-element.71), channel_id=1, source_target_pairs={{0,16},{4,20},{8,24},{12,28},{16,0},{20,4},{24,8},{28,12},{1,17},{... | collective-permute-start | bytes 786440 | tf_op jit(solution)/shard_map/ppermute | solution.py:169
  132.9 20.9 %collective-permute-start.7 = (bf16[4,256,128]{2,1,0:T(8,128)(2,1)S(1)}, bf16[4,256,128]{2,1,0:T(8,128)(2,1)S(1)}, u32[]{:S(2)}, u32[]{:S(2)}) collective-permute-start(bf16[4,256,128]{2,1,0:T(8,128)(2,1)S(1)} %get-tuple-element.64), channel_id=1, source_target_pairs={{0,12},{4,8},{8,4},{12,0},{16,28},{20,24},{24,20},{28,16},{1,13},{... | collective-permute-start | bytes 786440 | tf_op jit(solution)/shard_map/ppermute | solution.py:169
  135.0 18.8 %collective-permute-start.8 = (bf16[4,256,128]{2,1,0:T(8,128)(2,1)S(1)}, bf16[4,256,128]{2,1,0:T(8,128)(2,1)S(1)}, u32[]{:S(2)}, u32[]{:S(2)}) collective-permute-start(bf16[4,256,128]{2,1,0:T(8,128)(2,1)S(1)} %get-tuple-element.65), channel_id=1, source_target_pairs={{0,20},{4,16},{8,28},{12,24},{16,4},{20,0},{24,12},{28,8},{1,21},{... | collective-permute-start | bytes 786440 | tf_op jit(solution)/shard_map/ppermute | solution.py:169
  143.5 10.3 %collective-permute-start.9 = (bf16[4,256,128]{2,1,0:T(8,128)(2,1)S(1)}, bf16[4,256,128]{2,1,0:T(8,128)(2,1)S(1)}, u32[]{:S(2)}, u32[]{:S(2)}) collective-permute-start(bf16[4,256,128]{2,1,0:T(8,128)(2,1)S(1)} %get-tuple-element.66), channel_id=1, source_target_pairs={{0,4},{4,0},{8,12},{12,8},{16,20},{20,16},{24,28},{28,24},{1,5},{5... | collective-permute-start | bytes 786440 | tf_op jit(solution)/shard_map/ppermute | solution.py:169

commit v4 on v2

--- a/solution.py
+++ b/solution.py
@@ -54,6 +54,7 @@
         out_shape=low_array(owners, chans, 4, rows, HEAD_DIM),
         in_specs=[pl.BlockSpec((rows, owners * HEAD_DIM), lambda c: (0, c * turns + turn))] * 4,
         out_specs=pl.BlockSpec((owners, 1, 4, rows, HEAD_DIM), lambda c: (0, c, 0, 0, 0)),
+        compiler_params=pltpu.CompilerParams(vmem_limit_bytes=8 << 20) if turn else None,
         cost_estimate=moved(16 * rows * width // turns),
     )(*inputs)
 

time: 155 us -> 154 us (level)
  local copies, waits for them, and re-layouts: 3.34 us -> 1.69 us
    pallas_call x2, Pallas kernels: 7.96 us -> 6.1 us  [pack(): pl.pallas_call(functools.partial(pack_kernel, owners), grid=(chans,), out...]
    unnamed x6 -> x10, local copies, waits for them, and re-layouts: 2.89 us -> 1.23 us
where the time goes in v4:
time: 154 us; the launch traced here: 153 us
  waiting for transfers between devices  88.5 us (57%)
  Pallas kernels  31.5 us (20%)
  starting transfers between devices  28.3 us (18%)
  other arithmetic  1.82 us (1%)
  local copies, waits for them, and re-layouts  1.69 us (1%)
    ppermute x14, waiting for transfers between devices, exchange(): lax.ppermute(value, 'seq', [(s, s ^ d) for s in range(lax.axis_size('seq'...  45.5 us
    all_to_all x2, waiting for transfers between devices, gather(): lax.all_to_all(parts, ('seq', 'chan'), split_axis=0, concat_axis=0, tiled...  42.9 us
    pallas_call x2, Pallas kernels, attention(): pl.pallas_call(functools.partial(attention_kernel, spans), out_shape=[low...  21 us
    ppermute x14, starting transfers between devices, exchange(): lax.ppermute(value, 'seq', [(s, s ^ d) for s in range(lax.axis_size('seq'...  18.4 us
    all_to_all x2, starting transfers between devices, gather(): lax.all_to_all(parts, ('seq', 'chan'), split_axis=0, concat_axis=0, tiled...  9.93 us
    pallas_call x2, Pallas kernels, pack(): pl.pallas_call(functools.partial(pack_kernel, owners), grid=(chans,), out...  6.1 us
    pallas_call x4, Pallas kernels, unpack(): pl.pallas_call(functools.partial(unpack_kernel, peers, base), out_shape=[...  4.36 us
  transfers between devices with their start and end apart: 16, of which 10 were waited for; matrix products, arithmetic and copies ran while one was open for 1% of the time, Pallas kernels for 11%

profile of v4, /device:TPU:9, one launch (start us, length us, event | category | flops | bytes accessed | tf_op | source)
XLA Modules:
  0.0 152.8 jit_solution(17494727895555538803)
XLA Ops:
  0.6 4.0 %shard_map.85 = bf16[8,4,4,64,128]{4,3,2,1,0:T(8,128)(2,1)} custom-call(bf16[64,8192]{1,0:T(8,128)(2,1)} %refs_0_.3, bf16[64,8192]{1,0:T(8,128)(2,1)} %refs_1_.3, bf16[64,8192]{1,0:T(8,128)(2,1)} %refs_2_.3, bf16[64,8192]{1,0:T(8,128)(2,1)} %refs_3_.3), custom_call_target="tpu_custom_call" | custom-call | bytes 4194304 | tf_op jit(solution)/shard_map/pallas_call | solution.py:51
  4.6 6.4 %all-to-all-start = ((bf16[32,4,64,128]{3,2,1,0:T(8,128)(2,1)}), bf16[32,4,64,128]{3,2,1,0:T(8,128)(2,1)}, u32[]{:S(2)}, u32[]{:S(2)}) async-start(bf16[32,4,64,128]{3,2,1,0:T(8,128)(2,1)} %bitcast.7), calls=%async_computation | async-start | bytes 4194304 | tf_op jit(solution)/shard_map/all_to_all | solution.py:190
  11.1 1.2 copy-done.3
  12.3 2.1 %shard_map.84 = bf16[8,4,4,64,128]{4,3,2,1,0:T(8,128)(2,1)} custom-call(bf16[64,8192]{1,0:T(8,128)(2,1)S(1)} %copy-done, bf16[64,8192]{1,0:T(8,128)(2,1)S(1)} %copy-done.1, bf16[64,8192]{1,0:T(8,128)(2,1)S(1)} %copy-done.2, bf16[64,8192]{1,0:T(8,128)(2,1)S(1)} %copy-done.3), custom_call_target="tpu_custom_call" | custom-call | bytes 4194304 | tf_op jit(solution)/shard_map/pallas_call | solution.py:51
  14.4 1.8 %convert_reduce_fusion = s32[2048]{0:T(1024)S(1)} fusion(s32[2048]{0:T(1024)S(1)} %copy-done.4), kind=kLoop, calls=%fused_computation | loop fusion | flops 12580864 | bytes 16384 | tf_op jit(solution)/shard_map/reduce_sum | solution.py:181
  16.4 42.9 %all-to-all-done = bf16[32,4,64,128]{3,2,1,0:T(8,128)(2,1)} async-done(((bf16[32,4,64,128]{3,2,1,0:T(8,128)(2,1)}), bf16[32,4,64,128]{3,2,1,0:T(8,128)(2,1)}, u32[]{:S(2)}, u32[]{:S(2)}) %all-to-all-start) | async-done | bytes 2097184 | tf_op jit(solution)/shard_map/all_to_all | solution.py:190
  59.3 3.5 %all-to-all-start.1 = ((bf16[32,4,64,128]{3,2,1,0:T(8,128)(2,1)}), bf16[32,4,64,128]{3,2,1,0:T(8,128)(2,1)S(1)}, u32[]{:S(2)}, u32[]{:S(2)}) async-start(bf16[32,4,64,128]{3,2,1,0:T(8,128)(2,1)} %bitcast.4), calls=%async_computation.1 | async-start | bytes 4194304 | tf_op jit(solution)/shard_map/all_to_all | solution.py:190
  63.2 11.1 %shard_map.86 = (bf16[4,256,128]{2,1,0:T(8,128)(2,1)S(1)}, bf16[4,256,128]{2,1,0:T(8,128)(2,1)S(1)}, bf16[4,256,128]{2,1,0:T(8,128)(2,1)S(1)}, bf16[4,256,128]{2...) custom-call(s32[8]{0:T(128)S(1)} %subtract_add_fusion.count_ref, ...), custom_call_target="tpu_custom_call" | custom-call | flops 2415919104 | bytes 4194304 | tf_op jit(solution)/shard_map/pallas_call | solution.py:118
  74.2 2.2 %collective-permute-start.3 = (bf16[4,256,128]{2,1,0:T(8,128)(2,1)S(1)}, bf16[4,256,128]{2,1,0:T(8,128)(2,1)S(1)}, u32[]{:S(2)}, u32[]{:S(2)}) collective-permute-start(bf16[4,256,128]{2,1,0:T(8,128)(2,1)S(1)} %get-tuple-element.51), channel_id=1, source_target_pairs={{0,24},{4,28},{8,16},{12,20},{16,8},{20,12},{24,0},{28,4},{1,25},{... | collective-permute-start | bytes 786440 | tf_op jit(solution)/shard_map/ppermute | solution.py:169
  76.4 0.8 collective-permute-start.4
  77.2 0.9 collective-permute-start
  78.4 1.2 collective-permute-start.6
  79.6 7.5 %collective-permute-done.3.refs_1_ = bf16[4,256,128]{2,1,0:T(8,128)(2,1)S(1)} collective-permute-done((bf16[4,256,128]{2,1,0:T(8,128)(2,1)S(1)}, bf16[4,256,128]{2,1,0:T(8,128)(2,1)S(1)}, u32[]{:S(2)}, u32[]{:S(2)}) %collective-permute-start.3) | collective-permute-done | bytes 262176 | tf_op jit(solution)/shard_map/ppermute | solution.py:169
  87.1 3.5 %collective-permute-start.1 = (bf16[4,256,128]{2,1,0:T(8,128)(2,1)S(1)}, bf16[4,256,128]{2,1,0:T(8,128)(2,1)S(1)}, u32[]{:S(2)}, u32[]{:S(2)}) collective-permute-start(bf16[4,256,128]{2,1,0:T(8,128)(2,1)S(1)} %get-tuple-element.48), channel_id=1, source_target_pairs={{0,20},{4,16},{8,28},{12,24},{16,4},{20,0},{24,12},{28,8},{1,21},{... | collective-permute-start | bytes 786440 | tf_op jit(solution)/shard_map/ppermute | solution.py:169
  90.7 10.5 %collective-permute-done.4.refs_2_ = bf16[4,256,128]{2,1,0:T(8,128)(2,1)S(1)} collective-permute-done((bf16[4,256,128]{2,1,0:T(8,128)(2,1)S(1)}, bf16[4,256,128]{2,1,0:T(8,128)(2,1)S(1)}, u32[]{:S(2)}, u32[]{:S(2)}) %collective-permute-start.4) | collective-permute-done | bytes 262176 | tf_op jit(solution)/shard_map/ppermute | solution.py:169
  101.2 12.0 %collective-permute-done.5.refs_3_ = bf16[4,256,128]{2,1,0:T(8,128)(2,1)S(1)} collective-permute-done((bf16[4,256,128]{2,1,0:T(8,128)(2,1)S(1)}, bf16[4,256,128]{2,1,0:T(8,128)(2,1)S(1)}, u32[]{:S(2)}, u32[]{:S(2)}) %collective-permute-start.5) | collective-permute-done | bytes 262176 | tf_op jit(solution)/shard_map/ppermute | solution.py:169
  113.3 1.2 shard_map.87
  114.5 1.0 shard_map.88
  115.5 10.0 %shard_map.89 = (bf16[4,256,128]{2,1,0:T(8,128)(2,1)S(1)}, bf16[4,256,128]{2,1,0:T(8,128)(2,1)S(1)}, bf16[4,256,128]{2,1,0:T(8,128)(2,1)S(1)}, bf16[4,256,128]{2...) custom-call(s32[8]{0:T(128)S(1)} %subtract_add_fusion.count_ref, ...), custom_call_target="tpu_custom_call" | custom-call | flops 2415919104 | bytes 4194304 | tf_op jit(solution)/shard_map/pallas_call | solution.py:118
  125.5 1.7 %collective-permute-start.10 = (bf16[4,256,128]{2,1,0:T(8,128)(2,1)S(1)}, bf16[4,256,128]{2,1,0:T(8,128)(2,1)S(1)}, u32[]{:S(2)}, u32[]{:S(2)}) collective-permute-start(bf16[4,256,128]{2,1,0:T(8,128)(2,1)S(1)} %get-tuple-element.68), channel_id=1, source_target_pairs={{0,24},{4,28},{8,16},{12,20},{16,8},{20,12},{24,0},{28,4},{1,25},{... | collective-permute-start | bytes 786440 | tf_op jit(solution)/shard_map/ppermute | solution.py:169
  127.2 1.8 %collective-permute-start.11 = (bf16[4,256,128]{2,1,0:T(8,128)(2,1)S(1)}, bf16[4,256,128]{2,1,0:T(8,128)(2,1)S(1)}, u32[]{:S(2)}, u32[]{:S(2)}) collective-permute-start(bf16[4,256,128]{2,1,0:T(8,128)(2,1)S(1)} %get-tuple-element.69), channel_id=1, source_target_pairs={{0,28},{4,24},{8,20},{12,16},{16,12},{20,8},{24,4},{28,0},{1,29},{... | collective-permute-start | bytes 786440 | tf_op jit(solution)/shard_map/ppermute | solution.py:169
  129.0 1.2 collective-permute-start.12
  130.2 1.0 collective-permute-start.13
  131.2 2.3 %collective-permute-done.10.refs_1_ = bf16[4,256,128]{2,1,0:T(8,128)(2,1)S(1)} collective-permute-done((bf16[4,256,128]{2,1,0:T(8,128)(2,1)S(1)}, bf16[4,256,128]{2,1,0:T(8,128)(2,1)S(1)}, u32[]{:S(2)}, u32[]{:S(2)}) %collective-permute-start.10) | collective-permute-done | bytes 262176 | tf_op jit(solution)/shard_map/ppermute | solution.py:169
  133.4 3.8 %collective-permute-start.8 = (bf16[4,256,128]{2,1,0:T(8,128)(2,1)S(1)}, bf16[4,256,128]{2,1,0:T(8,128)(2,1)S(1)}, u32[]{:S(2)}, u32[]{:S(2)}) collective-permute-start(bf16[4,256,128]{2,1,0:T(8,128)(2,1)S(1)} %get-tuple-element.65), channel_id=1, source_target_pairs={{0,20},{4,16},{8,28},{12,24},{16,4},{20,0},{24,12},{28,8},{1,21},{... | collective-permute-start | bytes 786440 | tf_op jit(solution)/shard_map/ppermute | solution.py:169
  137.2 4.3 %collective-permute-done.11.refs_2_ = bf16[4,256,128]{2,1,0:T(8,128)(2,1)S(1)} collective-permute-done((bf16[4,256,128]{2,1,0:T(8,128)(2,1)S(1)}, bf16[4,256,128]{2,1,0:T(8,128)(2,1)S(1)}, u32[]{:S(2)}, u32[]{:S(2)}) %collective-permute-start.11) | collective-permute-done | bytes 262176 | tf_op jit(solution)/shard_map/ppermute | solution.py:169
  141.5 2.6 %collective-permute-done.12.refs_3_ = bf16[4,256,128]{2,1,0:T(8,128)(2,1)S(1)} collective-permute-done((bf16[4,256,128]{2,1,0:T(8,128)(2,1)S(1)}, bf16[4,256,128]{2,1,0:T(8,128)(2,1)S(1)}, u32[]{:S(2)}, u32[]{:S(2)}) %collective-permute-start.12) | collective-permute-done | bytes 262176 | tf_op jit(solution)/shard_map/ppermute | solution.py:169
  144.1 1.9 %collective-permute-done.13.refs_4_ = bf16[4,256,128]{2,1,0:T(8,128)(2,1)S(1)} collective-permute-done((bf16[4,256,128]{2,1,0:T(8,128)(2,1)S(1)}, bf16[4,256,128]{2,1,0:T(8,128)(2,1)S(1)}, u32[]{:S(2)}, u32[]{:S(2)}) %collective-permute-start.13) | collective-permute-done | bytes 262176 | tf_op jit(solution)/shard_map/ppermute | solution.py:169
  146.0 1.2 shard_map.90
  147.2 3.9 %collective-permute-done.7.refs_0_ = bf16[4,256,128]{2,1,0:T(8,128)(2,1)S(1)} collective-permute-done((bf16[4,256,128]{2,1,0:T(8,128)(2,1)S(1)}, bf16[4,256,128]{2,1,0:T(8,128)(2,1)S(1)}, u32[]{:S(2)}, u32[]{:S(2)}) %collective-permute-start.7) | collective-permute-done | bytes 262176 | tf_op jit(solution)/shard_map/ppermute | solution.py:169
  151.2 0.5 collective-permute-done.8.refs_1_
  151.6 1.0 shard_map.91
  (23 shorter events, 0.8 us)
Async XLA Ops:
  4.6 6.4 %copy-start = (bf16[64,8192]{1,0:T(8,128)(2,1)S(1)}, bf16[64,8192]{1,0:T(8,128)(2,1)}, u32[]{:S(2)}) copy-start(bf16[64,8192]{1,0:T(8,128)(2,1)} %refs_0_.3) | copy-start | bytes 3145732
  4.6 6.4 %copy-start.1 = (bf16[64,8192]{1,0:T(8,128)(2,1)S(1)}, bf16[64,8192]{1,0:T(8,128)(2,1)}, u32[]{:S(2)}) copy-start(bf16[64,8192]{1,0:T(8,128)(2,1)} %refs_1_.3) | copy-start | bytes 3145732
  4.6 6.5 %copy-start.2 = (bf16[64,8192]{1,0:T(8,128)(2,1)S(1)}, bf16[64,8192]{1,0:T(8,128)(2,1)}, u32[]{:S(2)}) copy-start(bf16[64,8192]{1,0:T(8,128)(2,1)} %refs_2_.3) | copy-start | bytes 3145732
  4.6 54.6 %all-to-all-start = ((bf16[32,4,64,128]{3,2,1,0:T(8,128)(2,1)}), bf16[32,4,64,128]{3,2,1,0:T(8,128)(2,1)}, u32[]{:S(2)}, u32[]{:S(2)}) async-start(bf16[32,4,64,128]{3,2,1,0:T(8,128)(2,1)} %bitcast.7), calls=%async_computation | async-start | bytes 4194304 | tf_op jit(solution)/shard_map/all_to_all | solution.py:190
  11.1 1.2 copy-start.3
  12.3 2.1 %copy-start.4 = (s32[2048]{0:T(1024)S(1)}, s32[2048]{0:T(1024)}, u32[]{:S(2)}) copy-start(s32[2048]{0:T(1024)} %param.5) | copy-start | bytes 24580
  59.3 56.2 %all-to-all-start.1 = ((bf16[32,4,64,128]{3,2,1,0:T(8,128)(2,1)}), bf16[32,4,64,128]{3,2,1,0:T(8,128)(2,1)S(1)}, u32[]{:S(2)}, u32[]{:S(2)}) async-start(bf16[32,4,64,128]{3,2,1,0:T(8,128)(2,1)} %bitcast.4), calls=%async_computation.1 | async-start | bytes 4194304 | tf_op jit(solution)/shard_map/all_to_all | solution.py:190
  74.2 12.9 %collective-permute-start.3 = (bf16[4,256,128]{2,1,0:T(8,128)(2,1)S(1)}, bf16[4,256,128]{2,1,0:T(8,128)(2,1)S(1)}, u32[]{:S(2)}, u32[]{:S(2)}) collective-permute-start(bf16[4,256,128]{2,1,0:T(8,128)(2,1)S(1)} %get-tuple-element.51), channel_id=1, source_target_pairs={{0,24},{4,28},{8,16},{12,20},{16,8},{20,12},{24,0},{28,4},{1,25},{... | collective-permute-start | bytes 786440 | tf_op jit(solution)/shard_map/ppermute | solution.py:169
  76.4 24.8 %collective-permute-start.4 = (bf16[4,256,128]{2,1,0:T(8,128)(2,1)S(1)}, bf16[4,256,128]{2,1,0:T(8,128)(2,1)S(1)}, u32[]{:S(2)}, u32[]{:S(2)}) collective-permute-start(bf16[4,256,128]{2,1,0:T(8,128)(2,1)S(1)} %get-tuple-element.52), channel_id=1, source_target_pairs={{0,28},{4,24},{8,20},{12,16},{16,12},{20,8},{24,4},{28,0},{1,29},{... | collective-permute-start | bytes 786440 | tf_op jit(solution)/shard_map/ppermute | solution.py:169
  77.2 37.3 %collective-permute-start = (bf16[4,256,128]{2,1,0:T(8,128)(2,1)S(1)}, bf16[4,256,128]{2,1,0:T(8,128)(2,1)S(1)}, u32[]{:S(2)}, u32[]{:S(2)}) collective-permute-start(bf16[4,256,128]{2,1,0:T(8,128)(2,1)S(1)} %get-tuple-element.47), channel_id=1, source_target_pairs={{0,12},{4,8},{8,4},{12,0},{16,28},{20,24},{24,20},{28,16},{1,13},{... | collective-permute-start | bytes 786440 | tf_op jit(solution)/shard_map/ppermute | solution.py:169
  78.1 35.1 %collective-permute-start.5 = (bf16[4,256,128]{2,1,0:T(8,128)(2,1)S(1)}, bf16[4,256,128]{2,1,0:T(8,128)(2,1)S(1)}, u32[]{:S(2)}, u32[]{:S(2)}) collective-permute-start(bf16[4,256,128]{2,1,0:T(8,128)(2,1)S(1)} %get-tuple-element.53), channel_id=1, source_target_pairs={{0,8},{4,12},{8,0},{12,4},{16,24},{20,28},{24,16},{28,20},{1,9},{5... | collective-permute-start | bytes 786440 | tf_op jit(solution)/shard_map/ppermute | solution.py:169
  78.4 34.8 %collective-permute-start.6 = (bf16[4,256,128]{2,1,0:T(8,128)(2,1)S(1)}, bf16[4,256,128]{2,1,0:T(8,128)(2,1)S(1)}, u32[]{:S(2)}, u32[]{:S(2)}) collective-permute-start(bf16[4,256,128]{2,1,0:T(8,128)(2,1)S(1)} %get-tuple-element.54), channel_id=1, source_target_pairs={{0,16},{4,20},{8,24},{12,28},{16,0},{20,4},{24,8},{28,12},{1,17},{... | collective-permute-start | bytes 786440 | tf_op jit(solution)/shard_map/ppermute | solution.py:169
  87.1 27.4 %collective-permute-start.1 = (bf16[4,256,128]{2,1,0:T(8,128)(2,1)S(1)}, bf16[4,256,128]{2,1,0:T(8,128)(2,1)S(1)}, u32[]{:S(2)}, u32[]{:S(2)}) collective-permute-start(bf16[4,256,128]{2,1,0:T(8,128)(2,1)S(1)} %get-tuple-element.48), channel_id=1, source_target_pairs={{0,20},{4,16},{8,28},{12,24},{16,4},{20,0},{24,12},{28,8},{1,21},{... | collective-permute-start | bytes 786440 | tf_op jit(solution)/shard_map/ppermute | solution.py:169
  101.2 13.3 %collective-permute-start.2 = (bf16[4,256,128]{2,1,0:T(8,128)(2,1)S(1)}, bf16[4,256,128]{2,1,0:T(8,128)(2,1)S(1)}, u32[]{:S(2)}, u32[]{:S(2)}) collective-permute-start(bf16[4,256,128]{2,1,0:T(8,128)(2,1)S(1)} %get-tuple-element.49), channel_id=1, source_target_pairs={{0,4},{4,0},{8,12},{12,8},{16,20},{20,16},{24,28},{28,24},{1,5},{5... | collective-permute-start | bytes 786440 | tf_op jit(solution)/shard_map/ppermute | solution.py:169
  125.5 7.9 %collective-permute-start.10 = (bf16[4,256,128]{2,1,0:T(8,128)(2,1)S(1)}, bf16[4,256,128]{2,1,0:T(8,128)(2,1)S(1)}, u32[]{:S(2)}, u32[]{:S(2)}) collective-permute-start(bf16[4,256,128]{2,1,0:T(8,128)(2,1)S(1)} %get-tuple-element.68), channel_id=1, source_target_pairs={{0,24},{4,28},{8,16},{12,20},{16,8},{20,12},{24,0},{28,4},{1,25},{... | collective-permute-start | bytes 786440 | tf_op jit(solution)/shard_map/ppermute | solution.py:169
  127.2 14.3 %collective-permute-start.11 = (bf16[4,256,128]{2,1,0:T(8,128)(2,1)S(1)}, bf16[4,256,128]{2,1,0:T(8,128)(2,1)S(1)}, u32[]{:S(2)}, u32[]{:S(2)}) collective-permute-start(bf16[4,256,128]{2,1,0:T(8,128)(2,1)S(1)} %get-tuple-element.69), channel_id=1, source_target_pairs={{0,28},{4,24},{8,20},{12,16},{16,12},{20,8},{24,4},{28,0},{1,29},{... | collective-permute-start | bytes 786440 | tf_op jit(solution)/shard_map/ppermute | solution.py:169
  129.0 15.2 %collective-permute-start.12 = (bf16[4,256,128]{2,1,0:T(8,128)(2,1)S(1)}, bf16[4,256,128]{2,1,0:T(8,128)(2,1)S(1)}, u32[]{:S(2)}, u32[]{:S(2)}) collective-permute-start(bf16[4,256,128]{2,1,0:T(8,128)(2,1)S(1)} %get-tuple-element.70), channel_id=1, source_target_pairs={{0,8},{4,12},{8,0},{12,4},{16,24},{20,28},{24,16},{28,20},{1,9},{5... | collective-permute-start | bytes 786440 | tf_op jit(solution)/shard_map/ppermute | solution.py:169
  130.2 15.8 %collective-permute-start.13 = (bf16[4,256,128]{2,1,0:T(8,128)(2,1)S(1)}, bf16[4,256,128]{2,1,0:T(8,128)(2,1)S(1)}, u32[]{:S(2)}, u32[]{:S(2)}) collective-permute-start(bf16[4,256,128]{2,1,0:T(8,128)(2,1)S(1)} %get-tuple-element.71), channel_id=1, source_target_pairs={{0,16},{4,20},{8,24},{12,28},{16,0},{20,4},{24,8},{28,12},{1,17},{... | collective-permute-start | bytes 786440 | tf_op jit(solution)/shard_map/ppermute | solution.py:169
  131.2 20.0 %collective-permute-start.7 = (bf16[4,256,128]{2,1,0:T(8,128)(2,1)S(1)}, bf16[4,256,128]{2,1,0:T(8,128)(2,1)S(1)}, u32[]{:S(2)}, u32[]{:S(2)}) collective-permute-start(bf16[4,256,128]{2,1,0:T(8,128)(2,1)S(1)} %get-tuple-element.64), channel_id=1, source_target_pairs={{0,12},{4,8},{8,4},{12,0},{16,28},{20,24},{24,20},{28,16},{1,13},{... | collective-permute-start | bytes 786440 | tf_op jit(solution)/shard_map/ppermute | solution.py:169
  133.4 18.2 %collective-permute-start.8 = (bf16[4,256,128]{2,1,0:T(8,128)(2,1)S(1)}, bf16[4,256,128]{2,1,0:T(8,128)(2,1)S(1)}, u32[]{:S(2)}, u32[]{:S(2)}) collective-permute-start(bf16[4,256,128]{2,1,0:T(8,128)(2,1)S(1)} %get-tuple-element.65), channel_id=1, source_target_pairs={{0,20},{4,16},{8,28},{12,24},{16,4},{20,0},{24,12},{28,8},{1,21},{... | collective-permute-start | bytes 786440 | tf_op jit(solution)/shard_map/ppermute | solution.py:169
  141.5 10.1 %collective-permute-start.9 = (bf16[4,256,128]{2,1,0:T(8,128)(2,1)S(1)}, bf16[4,256,128]{2,1,0:T(8,128)(2,1)S(1)}, u32[]{:S(2)}, u32[]{:S(2)}) collective-permute-start(bf16[4,256,128]{2,1,0:T(8,128)(2,1)S(1)} %get-tuple-element.66), channel_id=1, source_target_pairs={{0,4},{4,0},{8,12},{12,8},{16,20},{20,16},{24,28},{28,24},{1,5},{5... | collective-permute-start | bytes 786440 | tf_op jit(solution)/shard_map/ppermute | solution.py:169
